TPU v7x, 32 devices: a whole 2x2x4 slice. The times are simulated.
32 devices in a mesh: ex: 4 (over z), row: 2 (over core), col: 4 (over y, x).
Axes of the slice: x: 2, y: 2, z: 4, core: 2. Of those that a mesh axis runs over, the one named last changes fastest.
Arguments:
- tokens: bfloat16 [1536, 768], P(('ex', 'row')), may hold values from -6 to 6
- qkv_weight: bfloat16 [768, 2304], P('row', 'col'), may hold values from -0.21875 to 0.21875
- out_weight: bfloat16 [768, 768], P('col', 'row'), may hold values from -1 to 1
- bias_table: float32 [32, 12], P(None, 'col'), may hold values from -4 to 4
- first_norm_scale: float32 [768], replicated, may hold values from 0.5 to 1.5
- second_norm_scale: float32 [768], replicated, may hold values from 0.5 to 1.5
- router_weight: bfloat16 [768, 4], replicated, may hold values from -0.15625 to 0.15625
- expert_in: bfloat16 [4, 768, 3072], P('ex', None, ('row', 'col')), may hold values from -0.21875 to 0.21875
- expert_out: bfloat16 [4, 3072, 768], P('ex', ('row', 'col')), may hold values from -0.4375 to 0.4375
- lengths: int32 [4, 4], P('ex'), may hold values from 1 to 288, 384 in all within a row
- routes: int32 [1536], P(('ex', 'row')), may hold values from 0 to 3, as said below
- slots: int32 [1536], P(('ex', 'row')), may hold values from 0 to 15, as said below
- cotangent: bfloat16 [1536, 768], P(('ex', 'row')), may hold values from -6 to 6
Outputs:
- output: float32 [1536, 768], P(('ex', 'row', 'col'))
- input_grad: float32 [1536, 768], P(('ex', 'row', 'col'))
- qkv_grad: float32 [768, 2304], P('row', 'col')
- out_grad: float32 [768, 768], P('col', 'row')
- table_grad: float32 [32, 12], P(None, 'col')
- norm1_grad: float32 [768], replicated
- norm2_grad: float32 [768], replicated
- router_grad: float32 [768, 4], replicated
- expert_in_grad: float32 [4, 768, 3072], P('ex', None, ('row', 'col'))
- expert_out_grad: float32 [4, 3072, 768], P('ex', ('row', 'col'))
Inputs may be any that keep to these rules, and one draw needn't show every extreme that they name: `routes`: in each aligned block of 48 tokens no expert is named by more than 16 tokens, and some expert by exactly 16. `slots`: in each aligned block of 48 tokens no two tokens share both expert and slot. Each group's lengths sum to 384.
All inputs are finite; a program needn't handle non-finite values.
Results may differ from a plain program's by a relative error of at most 0.017.
Values may be sent and summed in bfloat16 or wider, within the bound.
A program may use at most 128 MiB of HBM per device.

v0:
```python
import jax
import jax.numpy as jnp
from jax import lax
from jax.sharding import PartitionSpec as P

HDIM = 64


EPS = 1e-06
NEG = -1e30
FAR_STEPS = (12, 16, 23, 32, 46, 64, 91)
HIGH = lax.Precision.HIGHEST
INNER = (((1,), (1,)), ((), ()))
OUTER = (((0,), (0,)), ((), ()))


def bucket_of(rel, buckets):
    dist = jnp.abs(rel)
    far = buckets // 4 + sum(((dist >= step).astype(jnp.int32) for step in FAR_STEPS))
    near = jnp.where(dist < buckets // 4, dist, far)
    return near + buckets // 2 * (rel > 0).astype(jnp.int32)


def toeplitz(vector, rows, cols):
    span = vector.shape[0]
    tiled = jnp.tile(vector, rows)[: rows * (span - 1)]
    return tiled.reshape(rows, span - 1)[:, :cols]


def diagonal_sums(matrix, span):
    rows, cols = matrix.shape
    padded = jnp.pad(matrix, ((0, 0), (0, span - 1 - cols))).reshape(-1)
    padded = jnp.pad(padded, (0, rows))
    return jnp.sum(padded.reshape(rows, span), axis=0)


def gelu_tanh(values):
    return jax.nn.gelu(values, approximate=True)


def on_device(
    tokens,
    qkv_weight,
    out_weight,
    bias_table,
    first_norm_scale,
    second_norm_scale,
    router_weight,
    expert_in,
    expert_out,
    lengths,
    routes,
    slots,
    cotangent,
):
    n_col = lax.axis_size("col")
    my_row = lax.axis_index("row")
    my_col = lax.axis_index("col")
    tokens_per_device, width = tokens.shape
    dispatch_mask = tokens_per_device // n_col
    experts = router_weight.shape[1]
    cap = max(2, (4 * dispatch_mask + 3 * experts - 1) // (3 * experts))
    heads = out_weight.shape[0] // HDIM
    buckets = bias_table.shape[0]
    scale = HDIM ** (-0.5)
    qkv_rows, out_rows, group_tokens = (
        lax.all_gather(qkv_weight, "row", axis=0, tiled=True),
        lax.all_gather(out_weight, "row", axis=1, tiled=True),
        lax.all_gather(tokens, "row", axis=0, tiled=True),
    )
    group = group_tokens.shape[0]
    local_offset = my_row * tokens_per_device
    quarter_offset = my_col * dispatch_mask
    full_sequence = group_tokens.astype(jnp.float32)
    first_inverse_norm = lax.rsqrt(
        jnp.mean(full_sequence * full_sequence, axis=1, keepdims=True) + EPS
    )
    first_unit_input = full_sequence * first_inverse_norm
    first_normed_input = (first_unit_input * first_norm_scale).astype(jnp.bfloat16)
    qkv = jnp.dot(first_normed_input, qkv_rows, preferred_element_type=jnp.float32).astype(
        jnp.bfloat16
    )
    qkv = qkv.reshape(group, heads, 3, HDIM).transpose(2, 1, 0, 3)
    queries = lax.dynamic_slice_in_dim(qkv[0], local_offset, tokens_per_device, 1)
    keys = qkv[1]
    values = qkv[2]
    ends = jnp.cumsum(lengths[0])
    places = jnp.arange(group, dtype=jnp.int32)
    segment = jnp.sum((places[:, None] >= ends[None, :]).astype(jnp.int32), axis=1)
    own_segment = lax.dynamic_slice_in_dim(segment, local_offset, tokens_per_device, 0)
    same = own_segment[:, None] == segment[None, :]
    span = tokens_per_device + group - 1
    offsets = jnp.arange(span, dtype=jnp.int32)
    shifts = jnp.where(offsets < group, offsets, offsets - span) - local_offset
    table_rows = (
        bucket_of(shifts, buckets)[:, None] == jnp.arange(buckets, dtype=jnp.int32)[None, :]
    ).astype(jnp.float32)
    bias_lines = jnp.dot(table_rows, bias_table, precision=HIGH).T

    def scores_of(query, key, line):
        raw = jnp.einsum(
            "qd,kd->qk", query, key, preferred_element_type=jnp.float32
        ) * scale + toeplitz(line, tokens_per_device, group)
        return jnp.where(same, raw, NEG)

    def attend(item):
        query, key, value, line = item
        masked = scores_of(query, key, line)
        top = jnp.max(masked, axis=1, keepdims=True)
        expo = jnp.exp(masked - top)
        total = jnp.sum(expo, axis=1, keepdims=True)
        weights = (expo / total).astype(jnp.bfloat16)
        mixed = jnp.dot(weights, value, preferred_element_type=jnp.float32)
        return (mixed, top + jnp.log(total))

    mixed, log_total = lax.map(attend, (queries, keys, values, bias_lines))
    attn = mixed.transpose(1, 0, 2).reshape(tokens_per_device, heads * HDIM).astype(jnp.bfloat16)
    branch = lax.psum_scatter(
        jnp.dot(attn, out_rows, preferred_element_type=jnp.float32),
        "col",
        scatter_dimension=0,
        tiled=True,
    )
    hidden_state = (
        lax.dynamic_slice_in_dim(tokens, quarter_offset, dispatch_mask, 0).astype(jnp.float32)
        + branch
    )
    second_inverse_norm = lax.rsqrt(
        jnp.mean(hidden_state * hidden_state, axis=1, keepdims=True) + EPS
    )
    second_unit_input = hidden_state * second_inverse_norm
    second_normed_input = (second_unit_input * second_norm_scale).astype(jnp.bfloat16)
    logits = jnp.dot(second_normed_input, router_weight, preferred_element_type=jnp.float32)
    peak = jnp.max(logits, axis=1, keepdims=True)
    raised = jnp.exp(logits - peak)
    gates = raised / jnp.sum(raised, axis=1, keepdims=True)
    route_here = lax.dynamic_slice_in_dim(routes, quarter_offset, dispatch_mask, 0)
    slot_here = lax.dynamic_slice_in_dim(slots, quarter_offset, dispatch_mask, 0)
    picks = (route_here[:, None] == jnp.arange(experts, dtype=jnp.int32)[None, :]).astype(
        jnp.float32
    )
    gate = jnp.sum(gates * picks, axis=1, keepdims=True)
    upstream = lax.dynamic_slice_in_dim(cotangent, quarter_offset, dispatch_mask, 0).astype(
        jnp.float32
    )
    scaled_grad = (gate * upstream).astype(jnp.bfloat16)
    place = route_here * cap + slot_here
    outbound = (
        jnp.zeros((experts * cap, width), jnp.bfloat16)
        .at[place]
        .set(second_normed_input)
        .reshape(experts, cap, width)
    )
    outbound_grad = (
        jnp.zeros((experts * cap, width), jnp.bfloat16)
        .at[place]
        .set(scaled_grad)
        .reshape(experts, cap, width)
    )
    arrived, arrived_grad = (
        lax.all_to_all(outbound, "ex", split_axis=0, concat_axis=0, tiled=True),
        lax.all_to_all(outbound_grad, "ex", split_axis=0, concat_axis=0, tiled=True),
    )
    arrived = arrived.reshape(experts * cap, width)
    arrived_grad = arrived_grad.reshape(experts * cap, width)
    inner, outer = (
        lax.all_gather(expert_in[0], ("row", "col"), axis=1, tiled=True),
        lax.all_gather(expert_out[0], ("row", "col"), axis=0, tiled=True),
    )
    pre = jnp.dot(arrived, inner, preferred_element_type=jnp.float32)
    activated, pull = jax.vjp(gelu_tanh, pre)
    hidden = activated.astype(jnp.bfloat16)
    expert_y = jnp.dot(hidden, outer, preferred_element_type=jnp.float32).astype(jnp.bfloat16)
    hidden_grad = lax.dot_general(arrived_grad, outer, INNER, preferred_element_type=jnp.float32)
    pre_grad = pull(hidden_grad)[0].astype(jnp.bfloat16)
    entry_grad = lax.dot_general(pre_grad, inner, INNER, preferred_element_type=jnp.float32).astype(
        jnp.bfloat16
    )
    inner_full = lax.dot_general(arrived, pre_grad, OUTER, preferred_element_type=jnp.float32)
    outer_full = lax.dot_general(hidden, arrived_grad, OUTER, preferred_element_type=jnp.float32)
    inner_grad, outer_grad = (
        lax.psum_scatter(
            inner_full.astype(jnp.bfloat16), ("row", "col"), scatter_dimension=1, tiled=True
        ).astype(jnp.float32),
        lax.psum_scatter(
            outer_full.astype(jnp.bfloat16), ("row", "col"), scatter_dimension=0, tiled=True
        ).astype(jnp.float32),
    )
    returned, returned_grad = (
        lax.all_to_all(
            expert_y.reshape(experts, cap, width), "ex", split_axis=0, concat_axis=0, tiled=True
        ),
        lax.all_to_all(
            entry_grad.reshape(experts, cap, width), "ex", split_axis=0, concat_axis=0, tiled=True
        ),
    )
    expert_back_rows = returned.reshape(experts * cap, width)[place].astype(jnp.float32)
    entry_back = returned_grad.reshape(experts * cap, width)[place].astype(jnp.float32)
    output = hidden_state + gate * expert_back_rows
    gate_grad = jnp.sum(upstream * expert_back_rows, axis=1, keepdims=True)
    logit_grad = gates * (picks * gate_grad - gate * gate_grad)
    router_part = jnp.dot(second_normed_input.astype(jnp.float32).T, logit_grad, precision=HIGH)
    second_normed_gradient = (
        jnp.dot(logit_grad, router_weight.astype(jnp.float32).T, precision=HIGH) + entry_back
    )
    second_norm_slice = jnp.sum(second_normed_gradient * second_unit_input, axis=0)
    second_scaled_input = second_norm_scale * second_normed_gradient
    state_grad = upstream + second_inverse_norm * (
        second_scaled_input
        - second_unit_input
        * jnp.mean(second_scaled_input * second_unit_input, axis=1, keepdims=True)
    )
    branch_all = lax.all_gather(state_grad.astype(jnp.bfloat16), "col", axis=0, tiled=True)
    out_full = lax.dot_general(attn, branch_all, OUTER, preferred_element_type=jnp.float32)
    attn_grad = lax.dot_general(
        branch_all, out_rows, INNER, preferred_element_type=jnp.float32
    ).astype(jnp.bfloat16)
    attn_grad = attn_grad.reshape(tokens_per_device, heads, HDIM).transpose(1, 0, 2)

    def attend_back(item):
        query, key, value, line, level, grad = item
        masked = scores_of(query, key, line)
        prob = jnp.exp(masked - level)
        weights = prob.astype(jnp.bfloat16)
        prob_grad = jnp.einsum("qd,kd->qk", grad, value, preferred_element_type=jnp.float32)
        value_grad = jnp.einsum("qk,qd->kd", weights, grad, preferred_element_type=jnp.float32)
        score_grad = (prob * (prob_grad - jnp.sum(prob_grad * prob, axis=1, keepdims=True))).astype(
            jnp.bfloat16
        )
        query_grad = jnp.dot(score_grad, key, preferred_element_type=jnp.float32) * scale
        key_grad = (
            jnp.einsum("qk,qd->kd", score_grad, query, preferred_element_type=jnp.float32) * scale
        )
        return (
            query_grad,
            key_grad,
            value_grad,
            diagonal_sums(score_grad.astype(jnp.float32), span),
        )

    query_grads, key_grads, value_grads, diagonals = lax.map(
        attend_back, (queries, keys, values, bias_lines, log_total, attn_grad)
    )
    key_cols = key_grads.transpose(1, 0, 2).reshape(group, heads * HDIM)
    value_cols = value_grads.transpose(1, 0, 2).reshape(group, heads * HDIM)
    key_own, value_own = (
        lax.psum_scatter(
            key_cols.astype(jnp.bfloat16), "row", scatter_dimension=0, tiled=True
        ).astype(jnp.float32),
        lax.psum_scatter(
            value_cols.astype(jnp.bfloat16), "row", scatter_dimension=0, tiled=True
        ).astype(jnp.float32),
    )
    stacked = jnp.stack(
        [
            query_grads.transpose(1, 0, 2),
            key_own.reshape(tokens_per_device, heads, HDIM),
            value_own.reshape(tokens_per_device, heads, HDIM),
        ],
        axis=2,
    )
    stacked = stacked.reshape(tokens_per_device, 3 * heads * HDIM).astype(jnp.bfloat16)
    xn_own = lax.dynamic_slice_in_dim(first_normed_input, local_offset, tokens_per_device, 0)
    local_unit_input = lax.dynamic_slice_in_dim(
        first_unit_input, local_offset, tokens_per_device, 0
    )
    qkv_full = lax.dot_general(xn_own, stacked, OUTER, preferred_element_type=jnp.float32)
    first_normed_slice = lax.dot_general(
        stacked, qkv_rows, INNER, preferred_element_type=jnp.float32
    )
    first_norm_slice = jnp.sum(first_normed_slice * local_unit_input, axis=0)
    table_part = jnp.dot(table_rows.T, diagonals.T, precision=HIGH)
    norm1_tiles = jnp.broadcast_to(first_norm_slice[None], (n_col, width))
    norm2_tiles = jnp.broadcast_to(second_norm_slice[None], (n_col, width))
    router_tiles = jnp.broadcast_to(router_part[None], (n_col, width, experts))
    xn_one_grad, norm1_cols, norm2_cols, router_cols = (
        lax.psum_scatter(
            first_normed_slice.astype(jnp.bfloat16), "col", scatter_dimension=0, tiled=True
        ).astype(jnp.float32),
        lax.psum_scatter(
            norm1_tiles.astype(jnp.bfloat16), "col", scatter_dimension=0, tiled=True
        ).astype(jnp.float32),
        lax.psum_scatter(
            norm2_tiles.astype(jnp.bfloat16), "col", scatter_dimension=0, tiled=True
        ).astype(jnp.float32),
        lax.psum_scatter(
            router_tiles.astype(jnp.bfloat16), "col", scatter_dimension=0, tiled=True
        ).astype(jnp.float32),
    )
    quarter_unit_input = lax.dynamic_slice_in_dim(
        local_unit_input, quarter_offset, dispatch_mask, 0
    )
    inv_quarter = lax.dynamic_slice_in_dim(
        first_inverse_norm, local_offset + quarter_offset, dispatch_mask, 0
    )
    first_scaled_input = first_norm_scale * xn_one_grad
    input_grad = state_grad + inv_quarter * (
        first_scaled_input
        - quarter_unit_input
        * jnp.mean(first_scaled_input * quarter_unit_input, axis=1, keepdims=True)
    )
    qkv_sum, out_sum, table_grad, norm1_grad, norm2_grad, router_grad = lax.psum(
        (qkv_full, out_full, table_part, norm1_cols[0], norm2_cols[0], router_cols[0]),
        ("ex", "row"),
    )
    half = width // lax.axis_size("row")
    qkv_grad = lax.dynamic_slice_in_dim(qkv_sum, my_row * half, half, 0)
    out_grad = lax.dynamic_slice_in_dim(out_sum, my_row * half, half, 1)
    return (
        output,
        input_grad,
        qkv_grad,
        out_grad,
        table_grad,
        norm1_grad,
        norm2_grad,
        router_grad,
        inner_grad[None],
        outer_grad[None],
    )


def solution(mesh):
    return jax.shard_map(
        on_device,
        mesh=mesh,
        in_specs=(
            P(("ex", "row"), None),
            P("row", "col"),
            P("col", "row"),
            P(None, "col"),
            P(),
            P(),
            P(),
            P("ex", None, ("row", "col")),
            P("ex", ("row", "col"), None),
            P("ex", None),
            P(("ex", "row")),
            P(("ex", "row")),
            P(("ex", "row"), None),
        ),
        out_specs=(
            P(("ex", "row", "col"), None),
            P(("ex", "row", "col"), None),
            P("row", "col"),
            P("col", "row"),
            P(None, "col"),
            P(),
            P(),
            P(),
            P("ex", None, ("row", "col")),
            P("ex", ("row", "col"), None),
        ),
        check_vma=False,
    )
```

profile of v0, /device:TPU:0, one launch (start us, length us, event | category | flops | bytes accessed | tf_op | source)
XLA Modules:
  0.0 422.1 jit_solution(4735138818069941916)
XLA Ops:
  8.1 2.5 all_gather.18
  10.9 2.7 all_gather.19
  17.2 8.1 %while.32 = (s32[]{:T(128)}, bf16[3,192,64]{1,2,0:T(8,128)(2,1)S(1)}, f32[3,192,1]{1,2,0:T(1,128)S(1)}, bf16[3,192,64]{2,1,0:T(8,128)(2,1)S(1)}, bf16[3,384,64]{...) while((s32[]{:T(128)}, ...), condition=%wide.region_6.7_spmd.clone, body=%wide.region_3.6_spmd.clone.sunk | while | flops 19611456 | bytes 3718249 | solution.py:116
  25.3 2.3 all_gather.20
  30.0 44.1 %reduce-scatter.13.cloned.1.call-done = f32[48,768]{1,0:T(8,128)} async-done(((f32[192,768]{1,0:T(8,128)}), f32[48,768]{1,0:T(8,128)}) %reduce-scatter.13.cloned.1.call-update) | async-done | bytes 147472 | tf_op jit(solution)/shard_map/reduce_scatter | solution.py:118
  75.2 1.5 scatter_custom_fusion
  76.7 4.6 %all-to-all-start = ((bf16[4,16,768]{2,1,0:T(8,128)(2,1)}), bf16[4,16,768]{2,1,0:T(8,128)(2,1)S(1)}, u32[]{:S(2)}, u32[]{:S(2)}) async-start(bf16[4,16,768]{2,1,0:T(8,128)(2,1)} %bitcast.10), calls=%async_computation.1 | async-start | bytes 196608 | tf_op jit(solution)/shard_map/all_to_all | solution.py:161
  81.6 1.5 scatter_custom_fusion.1
  83.1 4.0 all-to-all-done
  87.1 3.3 all-to-all-start.2
  90.5 3.3 fusion.54
  93.8 2.5 all-to-all-done.2
  96.3 18.8 %all-gather.7.cloned.1.call-done = bf16[1,3072,768]{2,1,0:T(8,128)(2,1)} async-done(((bf16[1,384,768]{2,1,0:T(8,128)(2,1)}), bf16[1,3072,768]{2,1,0:T(8,128)(2,1)}) %all-gather.7.cloned.1.call-update) | async-done | bytes 4718608 | tf_op jit(solution)/shard_map/all_gather | solution.py:168
  115.0 4.1 fusion.69
  119.2 2.2 fusion.57
  121.4 4.6 %all-to-all-start.3 = ((bf16[4,16,768]{2,1,0:T(8,128)(2,1)}), bf16[4,16,768]{2,1,0:T(8,128)(2,1)S(1)}, u32[]{:S(2)}, u32[]{:S(2)}) async-start(bf16[4,16,768]{2,1,0:T(8,128)(2,1)} %bitcast.18), calls=%async_computation.4 | async-start | bytes 196608 | tf_op jit(solution)/shard_map/all_to_all | solution.py:193
  126.0 4.0 fusion.60
  130.0 1.9 all-to-all-done.3
  131.9 3.3 all-to-all-start.1
  136.0 5.0 %all-to-all-done.1 = bf16[4,16,768]{2,1,0:T(8,128)(2,1)S(1)} async-done(((bf16[4,16,768]{2,1,0:T(8,128)(2,1)}), bf16[4,16,768]{2,1,0:T(8,128)(2,1)S(1)}, u32[]{:S(2)}, u32[]{:S(2)}) %all-to-all-start.1) | async-done | bytes 98336 | tf_op jit(solution)/shard_map/all_to_all | solution.py:190
  143.0 9.3 %all_gather.23 = bf16[192,768]{1,0:T(8,128)(2,1)S(1)} all-gather(bf16[48,768]{1,0:T(8,128)(2,1)S(1)} %fusion.113), channel_id=1, replica_groups=mesh['ex'=4,'row'=2,'col'=4] {'col'}, dimensions={0}, use_global_device_ids=true | all-gather | bytes 368640 | tf_op jit(solution)/shard_map/all_gather | solution.py:213
  154.7 25.0 %while.33 = (s32[]{:T(128)}, bf16[3,192,64]{1,2,0:T(8,128)(2,1)}, bf16[3,384,64]{1,2,0:T(8,128)(2,1)}, bf16[3,384,64]{1,2,0:T(8,128)(2,1)}, f32[3,575]{1,0:T(4,1...) while((s32[]{:T(128)}, bf16[3,192,64]{1,2,0:T(8,128)(2,1)}, ...), condition=%wide.region_19.20_spmd.clone, body=%wide.region_16.19_spmd.clone.sunk | while | flops 48253824 | bytes 8293271 | solution.py:241
  155.9 1.2 multiply_reduce_fusion.7
  159.0 1.6 fusion.176
  161.7 1.3 dynamic_update_slice.56
  167.3 1.6 fusion.176
  170.0 1.3 dynamic_update_slice.56
  175.6 1.6 fusion.176
  178.3 1.3 dynamic_update_slice.56
  179.7 1.8 copy.36
  181.5 1.7 copy.34
  183.3 3.6 reduce-scatter.21.cloned.1.call-done
  188.0 10.1 %reduce-scatter.19.cloned.1.call-done = bf16[192,192]{1,0:T(8,128)(2,1)} async-done(((bf16[384,192]{1,0:T(8,128)(2,1)}), bf16[192,192]{1,0:T(8,128)(2,1)}) %reduce-scatter.19.cloned.1.call-update) | async-done | bytes 73744
  200.0 2.3 multiply_reduce_fusion.1
  203.5 2.6 fusion.72
  206.2 3.6 convolution_convert_fusion.1
  209.8 6.6 %copy.38 = bf16[768,3072]{0,1:T(8,128)(2,1)} copy(bf16[768,3072]{1,0:T(8,128)(2,1)} %convolution_convert_fusion.1) | data formatting | bytes 9437184
  217.3 3.6 convolution_convert_fusion
  222.7 16.8 %all-reduce.7 = (bf16[4,768]{1,0:T(4,128)(2,1)S(1)}, bf16[4,768]{1,0:T(4,128)(2,1)S(1)}, bf16[4,768,4]{1,2,0:T(4,128)(2,1)S(1)}) all-reduce(bf16[4,768]{1,0:T(4,128)(2,1)S(1)} %broadcast_in_dim.110, bf16[4,768]{1,0:T(4,128)(2,1)S(1)} %broadcast_in_dim.111, ...), channel_id=8, replica_groups=mesh['ex'=4,'row'=2,'col'=4] {'col'}, use_global_device_ids=true, to_apply=%region_28.29.clone | all-reduce | flops 18432 | bytes 73728
  240.8 27.2 %all-reduce.5 = (f32[32,3]{0,1:T(4,128)}, f32[768]{0:T(1024)}, f32[768]{0:T(1024)}, f32[768,4]{0,1:T(4,128)}) all-reduce(f32[32,3]{0,1:T(4,128)S(1)} %fusion.74, f32[768]{0:T(1024)S(1)} %get-tuple-element.342, f32[768]{0:T(1024)S(1)} %get-tuple-element.341, ...), channel_id=1, replica_groups=mesh['ex'=4,'row'=2,'col'=4] {'ex','row'}, use_global_device_ids=true, to_apply=%region_26.27 | all-reduce | flops 4704 | bytes 37632 | tf_op jit(solution)/shard_map/psum | solution.py:302
  269.1 1.8 multiply_add_fusion
  270.9 27.5 %all-reduce.10.cloned.1.call-done = (f32[768,576]{0,1:T(8,128)}, f32[192,768]{1,0:T(8,128)}) async-done(((f32[768,576]{0,1:T(8,128)}, f32[192,768]{1,0:T(8,128)}), (f32[768,576]{0,1:T(8,128)}, f32[192,768]{1,0:T(8,128)})) %all-reduce.10.cloned.1.call-update) | async-done | bytes 2359312 | tf_op jit(solution)/shard_map/psum | solution.py:302
  298.4 1.7 constant_dynamic-slice_fusion.1
  300.1 2.1 constant_dynamic-slice_fusion.2
  302.2 52.9 %reduce-scatter.23.cloned.1.call-done = bf16[384,768]{1,0:T(8,128)(2,1)} async-done(((bf16[3072,768]{1,0:T(8,128)(2,1)}), bf16[384,768]{1,0:T(8,128)(2,1)}) %reduce-scatter.23.cloned.1.call-update) | async-done | bytes 589840
  355.1 1.4 copy.39
  357.6 54.9 %reduce-scatter.17.cloned.1.call-done = bf16[384,768]{1,0:T(8,128)(2,1)} async-done(((bf16[3072,768]{1,0:T(8,128)(2,1)}), bf16[384,768]{1,0:T(8,128)(2,1)}) %reduce-scatter.17.cloned.1.call-update) | async-done | bytes 589840 | tf_op jit(solution)/shard_map/reduce_scatter | solution.py:185
  412.5 2.2 bitcast_convert_fusion
  (217 shorter events, 45.5 us)
Async XLA Ops:
  8.0 73.4 %copy-start = (bf16[768,4]{0,1:T(4,128)(2,1)S(1)}, bf16[768,4]{0,1:T(4,128)(2,1)}, u32[]{:S(2)}) copy-start(bf16[768,4]{0,1:T(4,128)(2,1)} %param.23) | copy-start | bytes 18436
  8.0 66.1 %reduce-scatter.13.cloned.1.call-start = ((), (), s32[]{:S(2)}) async-start(), calls=%async_computation.10 | async-start | bytes 737280 | tf_op jit(solution)/shard_map/reduce_scatter | solution.py:118
  8.1 8.7 %copy-start.23 = (s32[575]{0:T(1024)}, s32[575]{0:T(1024)S(1)}, u32[]{:S(2)}) copy-start(s32[575]{0:T(1024)S(1)} %fusion.88) | copy-start | bytes 6904
  10.6 5.8 %copy-start.33 = (s32[1,4]{1,0:T(1,128)S(1)}, s32[1,4]{1,0:T(1,128)}, u32[]{:S(2)}) copy-start(s32[1,4]{1,0:T(1,128)} %param.26) | copy-start | bytes 52
  10.8 5.9 %copy-start.32 = (f32[32,3]{0,1:T(4,128)S(1)}, f32[32,3]{0,1:T(4,128)}, u32[]{:S(2)}) copy-start(f32[32,3]{0,1:T(4,128)} %param.20) | copy-start | bytes 1156
  13.5 1.6 copy-start.2
  14.4 0.8 copy-start.7
  17.1 12.8 %copy-start.29 = (s32[192]{0:T(256)S(1)}, s32[192]{0:T(256)}, u32[]{:S(2)}) copy-start(s32[192]{0:T(256)} %param.27) | copy-start | bytes 2308
  17.2 12.8 %copy-start.30 = (s32[192]{0:T(256)S(1)}, s32[192]{0:T(256)}, u32[]{:S(2)}) copy-start(s32[192]{0:T(256)} %param.28) | copy-start | bytes 2308
  17.2 58.1 %copy-start.21 = (f32[768]{0:T(1024)S(1)}, f32[768]{0:T(1024)}, u32[]{:S(2)}) copy-start(f32[768]{0:T(1024)} %param.22) | copy-start | bytes 9220
  17.2 64.4 %copy-start.20 = (bf16[192,768]{1,0:T(8,128)(2,1)S(1)}, bf16[192,768]{1,0:T(8,128)(2,1)}, u32[]{:S(2)}) copy-start(bf16[192,768]{1,0:T(8,128)(2,1)} %param.29) | copy-start | bytes 884740
  25.3 4.7 %copy-start.12 = (bf16[3,192,64]{1,2,0:T(8,128)(2,1)}, bf16[3,192,64]{1,2,0:T(8,128)(2,1)S(1)}, u32[]{:S(2)}) copy-start(bf16[3,192,64]{1,2,0:T(8,128)(2,1)S(1)} %get-tuple-element.205) | copy-start | bytes 221188
  28.7 61.8 %all-gather.5.cloned.1.call-start = ((), (), s32[]{:S(2)}) async-start(), calls=%async_computation.13 | async-start | bytes 5308416 | tf_op jit(solution)/shard_map/all_gather | solution.py:167
  29.3 85.7 %all-gather.7.cloned.1.call-start = ((), (), s32[]{:S(2)}) async-start(), calls=%async_computation.14 | async-start | bytes 5308416 | tf_op jit(solution)/shard_map/all_gather | solution.py:168
  76.7 10.4 %all-to-all-start = ((bf16[4,16,768]{2,1,0:T(8,128)(2,1)}), bf16[4,16,768]{2,1,0:T(8,128)(2,1)S(1)}, u32[]{:S(2)}, u32[]{:S(2)}) async-start(bf16[4,16,768]{2,1,0:T(8,128)(2,1)} %bitcast.10), calls=%async_computation.1 | async-start | bytes 196608 | tf_op jit(solution)/shard_map/all_to_all | solution.py:161
  81.4 37.8 %copy-start.16 = (bf16[48,768]{1,0:T(8,128)(2,1)}, bf16[48,768]{1,0:T(8,128)(2,1)S(1)}, u32[]{:S(2)}) copy-start(bf16[48,768]{1,0:T(8,128)(2,1)S(1)} %multiply_convert_fusion.3) | copy-start | bytes 221188
  87.1 32.0 %copy-start.10 = (bf16[4,16,768]{2,1,0:T(8,128)(2,1)}, bf16[4,16,768]{2,1,0:T(8,128)(2,1)S(1)}, u32[]{:S(2)}) copy-start(bf16[4,16,768]{2,1,0:T(8,128)(2,1)S(1)} %all-to-all-done) | copy-start | bytes 294916
  87.1 9.1 %all-to-all-start.2 = ((bf16[4,16,768]{2,1,0:T(8,128)(2,1)}), bf16[4,16,768]{2,1,0:T(8,128)(2,1)S(1)}, u32[]{:S(2)}, u32[]{:S(2)}) async-start(bf16[4,16,768]{2,1,0:T(8,128)(2,1)} %bitcast.16), calls=%async_computation.3 | async-start | bytes 196608 | tf_op jit(solution)/shard_map/all_to_all | solution.py:162
  96.3 25.2 %copy-start.18 = (bf16[4,16,768]{2,1,0:T(8,128)(2,1)}, bf16[4,16,768]{2,1,0:T(8,128)(2,1)S(1)}, u32[]{:S(2)}) copy-start(bf16[4,16,768]{2,1,0:T(8,128)(2,1)S(1)} %all-to-all-done.2) | copy-start | bytes 294916
  115.0 4.2 copy-start.1
  119.2 2.2 copy-start.5
  121.4 10.5 %all-to-all-start.3 = ((bf16[4,16,768]{2,1,0:T(8,128)(2,1)}), bf16[4,16,768]{2,1,0:T(8,128)(2,1)S(1)}, u32[]{:S(2)}, u32[]{:S(2)}) async-start(bf16[4,16,768]{2,1,0:T(8,128)(2,1)} %bitcast.18), calls=%async_computation.4 | async-start | bytes 196608 | tf_op jit(solution)/shard_map/all_to_all | solution.py:193
  131.9 9.1 %all-to-all-start.1 = ((bf16[4,16,768]{2,1,0:T(8,128)(2,1)}), bf16[4,16,768]{2,1,0:T(8,128)(2,1)S(1)}, u32[]{:S(2)}, u32[]{:S(2)}) async-start(bf16[4,16,768]{2,1,0:T(8,128)(2,1)} %bitcast.14), calls=%async_computation.2 | async-start | bytes 196608 | tf_op jit(solution)/shard_map/all_to_all | solution.py:190
  135.2 51.7 %reduce-scatter.21.cloned.1.call-start = ((), (), s32[]{:S(2)}) async-start(), calls=%async_computation.16 | async-start | bytes 294912
  141.7 13.0 %copy-start.14 = (bf16[48,768]{1,0:T(8,128)(2,1)}, bf16[48,768]{1,0:T(8,128)(2,1)S(1)}, u32[]{:S(2)}) copy-start(bf16[48,768]{1,0:T(8,128)(2,1)S(1)} %gather_fusion) | copy-start | bytes 221188
  141.8 12.9 %copy-start.25 = (f32[48]{0:T(128)}, f32[48]{0:T(128)S(1)}, u32[]{:S(2)}) copy-start(f32[48]{0:T(128)S(1)} %mul.254) | copy-start | bytes 580
  142.3 0.7 copy-start.8
  142.3 12.5 %copy-start.27 = (f32[48]{0:T(128)}, f32[48]{0:T(128)S(1)}, u32[]{:S(2)}) copy-start(f32[48]{0:T(128)S(1)} %broadcast_multiply_fusion.1) | copy-start | bytes 580
  152.3 0.7 copy-start.3
  179.7 22.8 %copy-start.4 = (bf16[192,768]{1,0:T(8,128)(2,1)S(1)}, bf16[192,768]{1,0:T(8,128)(2,1)}, u32[]{:S(2)}) copy-start(bf16[192,768]{1,0:T(8,128)(2,1)} %copy-done.3) | copy-start | bytes 884740
  179.7 22.8 %copy-start.13 = (bf16[3,192,64]{1,2,0:T(8,128)(2,1)S(1)}, bf16[3,192,64]{1,2,0:T(8,128)(2,1)}, u32[]{:S(2)}) copy-start(bf16[3,192,64]{1,2,0:T(8,128)(2,1)} %copy-done.12) | copy-start | bytes 221188
  181.5 16.6 %reduce-scatter.19.cloned.1.call-start = ((), (), s32[]{:S(2)}) async-start(), calls=%async_computation.15 | async-start | bytes 294912
  183.3 84.8 %reduce-scatter.15.cloned.1.call-start = ((), (), s32[]{:S(2)}) async-start(), calls=%async_computation.11 | async-start | bytes 368640 | tf_op jit(solution)/shard_map/reduce_scatter | solution.py:277
  188.0 18.2 %copy-start.6 = (bf16[64,3072]{1,0:T(8,128)(2,1)S(1)}, bf16[64,3072]{1,0:T(8,128)(2,1)}, u32[]{:S(2)}) copy-start(bf16[64,3072]{1,0:T(8,128)(2,1)} %copy-done.5) | copy-start | bytes 1179652
  188.0 18.2 %copy-start.11 = (bf16[4,16,768]{2,1,0:T(8,128)(2,1)S(1)}, bf16[4,16,768]{2,1,0:T(8,128)(2,1)}, u32[]{:S(2)}) copy-start(bf16[4,16,768]{2,1,0:T(8,128)(2,1)} %copy-done.10) | copy-start | bytes 294916
  202.4 96.0 %all-reduce.10.cloned.1.call-start = ((), (), s32[]{:S(2)}) async-start(), calls=%async_computation.18 | async-start | bytes 4718592 | tf_op jit(solution)/shard_map/psum | solution.py:302
  206.1 149.0 %reduce-scatter.23.cloned.1.call-start = ((), (), s32[]{:S(2)}) async-start(), calls=%async_computation.17 | async-start | bytes 5308416
  216.4 0.9 copy-start.19
  216.4 196.0 %reduce-scatter.17.cloned.1.call-start = ((), (), s32[]{:S(2)}) async-start(), calls=%async_computation.12 | async-start | bytes 5308416 | tf_op jit(solution)/shard_map/reduce_scatter | solution.py:185
  220.9 0.7 copy-start.34
  220.9 1.2 copy-start.24
  220.9 1.2 copy-start.31
  220.9 1.5 copy-start.17
  220.9 1.5 copy-start.26
  220.9 47.1 %copy-start.22 = (f32[768]{0:T(1024)S(1)}, f32[768]{0:T(1024)}, u32[]{:S(2)}) copy-start(f32[768]{0:T(1024)} %param.21) | copy-start | bytes 9220
  221.0 48.1 %copy-start.9 = (f32[48,768]{1,0:T(8,128)S(1)}, f32[48,768]{1,0:T(8,128)}, u32[]{:S(2)}) copy-start(f32[48,768]{1,0:T(8,128)} %copy-done.8) | copy-start | bytes 442372
  221.0 48.1 %copy-start.15 = (bf16[48,768]{1,0:T(8,128)(2,1)S(1)}, bf16[48,768]{1,0:T(8,128)(2,1)}, u32[]{:S(2)}) copy-start(bf16[48,768]{1,0:T(8,128)(2,1)} %copy-done.14) | copy-start | bytes 221188
  221.0 48.1 %copy-start.28 = (f32[48]{0:T(128)S(1)}, f32[48]{0:T(128)}, u32[]{:S(2)}) copy-start(f32[48]{0:T(128)} %copy-done.27) | copy-start | bytes 580
Sparse Core Ops, SparseCore 0:
  28.8 45.2 reduce-scatter.12
  181.6 5.3 reduce-scatter.20
  189.3 8.7 reduce-scatter.18
  202.5 25.4 reduce-scatter.14
  231.0 67.2 all-reduce.9
  302.1 52.9 reduce-scatter.22
  358.5 53.8 reduce-scatter.16
Sparse Core Ops, SparseCore 1:
  31.2 43.1 all-gather.4
  76.2 38.7 all-gather.6
where the time goes:
time: 424 us; the launch traced here: 422 us
  waiting for transfers between devices  227 us (54%)
  blocking collectives  60.7 us (14%)
  matrix products  48.8 us (12%)
  local copies, waits for them, and re-layouts  37.7 us (9%)
  starting transfers between devices  16.2 us (4%)
  between operations  16.2 us (4%)
  other arithmetic  15.4 us (4%)
    unnamed x12, waiting for transfers between devices  67.8 us
    reduce_scatter x1, waiting for transfers between devices, on_device(): lax.psum_scatter(outer_full.astype(jnp.bfloat16), ('row', 'col'), scatter...  54.9 us
    reduce_scatter x1, waiting for transfers between devices, on_device(): lax.psum_scatter(jnp.dot(attn, out_rows, preferred_element_type=jnp.float...  44.1 us
    psum x1, waiting for transfers between devices, on_device(): lax.psum((qkv_full, out_full, table_part, norm1_cols[0], norm2_cols[0], r...  27.5 us
    psum x1, blocking collectives, on_device(): lax.psum((qkv_full, out_full, table_part, norm1_cols[0], norm2_cols[0], r...  27.2 us
    all_gather x1, waiting for transfers between devices, on_device(): lax.all_gather(expert_out[0], ('row', 'col'), axis=0, tiled=True)  18.8 us
    unnamed x77, local copies, waits for them, and re-layouts  17 us
    unnamed x1, blocking collectives  16.8 us
  transfers between devices with their start and end apart: 13, of which 11 were waited for; matrix products, arithmetic and copies ran while one was open for 10% of the time, Pallas kernels for 0%

commit v1 on v0

--- a/solution.py
+++ b/solution.py
@@ -1,6 +1,8 @@
 import jax
 import jax.numpy as jnp
 from jax import lax
+from jax.experimental import pallas as pl
+from jax.experimental.pallas import tpu as pltpu
 from jax.sharding import PartitionSpec as P
 
 HDIM = 64
@@ -36,6 +38,439 @@
 
 def gelu_tanh(values):
     return jax.nn.gelu(values, approximate=True)
+
+
+VMEM = pl.BlockSpec(memory_space=pltpu.VMEM)
+DMA = pltpu.SemaphoreType.DMA
+VMEM_LIMIT = 48 * 1024 * 1024
+
+
+def params(collective):
+    return pltpu.CompilerParams(
+        collective_id=collective, has_side_effects=True, vmem_limit_bytes=VMEM_LIMIT
+    )
+
+
+def remote(src, dst, send, recv, device):
+    return pltpu.make_async_remote_copy(
+        src_ref=src,
+        dst_ref=dst,
+        send_sem=send,
+        recv_sem=recv,
+        device_id=device,
+        device_id_type=pl.DeviceIdType.MESH,
+    )
+
+
+def greet(peers):
+    barrier = pltpu.get_barrier_semaphore()
+    for peer in peers:
+        pl.semaphore_signal(
+            barrier, inc=1, device_id=peer, device_id_type=pl.DeviceIdType.MESH
+        )
+    pl.semaphore_wait(barrier, len(peers))
+
+
+def others(axis):
+    size = lax.axis_size(axis)
+    me = lax.axis_index(axis)
+    return [lax.rem(me + k, size) for k in range(1, size)]
+
+
+def gather_blocks(block, axis, collective):
+    size = lax.axis_size(axis)
+
+    def kernel(x, out, send, recv):
+        me = lax.axis_index(axis)
+        peers = others(axis)
+        greet([{axis: p} for p in peers])
+        copies = [
+            remote(x, out.at[me], send.at[k], recv.at[k], {axis: p}) for k, p in enumerate(peers)
+        ]
+        for copy in copies:
+            copy.start()
+        out[me] = x[...]
+        for copy in copies:
+            copy.wait()
+
+    return pl.pallas_call(
+        kernel,
+        out_shape=jax.ShapeDtypeStruct((size, *block.shape), block.dtype),
+        in_specs=[VMEM],
+        out_specs=VMEM,
+        scratch_shapes=[DMA((size - 1,)), DMA((size - 1,))],
+        compiler_params=params(collective),
+    )(block)
+
+
+def scatter_sum(blocks, axis, collective):
+    size = lax.axis_size(axis)
+
+    def kernel(x, out, land, send, recv):
+        me = lax.axis_index(axis)
+        peers = others(axis)
+        greet([{axis: p} for p in peers])
+        copies = [
+            remote(x.at[p], land.at[k], send.at[k], recv.at[k], {axis: p})
+            for k, p in enumerate(peers)
+        ]
+        for copy in copies:
+            copy.start()
+        total = x[me].astype(jnp.float32)
+        for k, copy in enumerate(copies):
+            copy.wait_recv()
+            total = total + land[k].astype(jnp.float32)
+        out[...] = total
+        for copy in copies:
+            copy.wait_send()
+
+    return pl.pallas_call(
+        kernel,
+        out_shape=jax.ShapeDtypeStruct(blocks.shape[1:], jnp.float32),
+        in_specs=[VMEM],
+        out_specs=VMEM,
+        scratch_shapes=[
+            pltpu.VMEM((size - 1, *blocks.shape[1:]), blocks.dtype),
+            DMA((size - 1,)),
+            DMA((size - 1,)),
+        ],
+        compiler_params=params(collective),
+    )(blocks)
+
+
+def gather_row(qkv_weight, out_weight, tokens):
+    rows, qkv_cols = qkv_weight.shape
+    head_rows, half = out_weight.shape
+    count, width = tokens.shape
+
+    def kernel(w, o, t, wf, of, tf, send, recv):
+        me = lax.axis_index("row")
+        peer = {"row": 1 - me}
+        greet([peer])
+        own_w = wf.at[pl.ds(pl.multiple_of(me * rows, rows), rows)]
+        own_o = of.at[:, pl.ds(pl.multiple_of(me * half, half), half)]
+        own_t = tf.at[pl.ds(pl.multiple_of(me * count, count), count)]
+        copies = [
+            remote(t, own_t, send.at[0], recv.at[0], peer),
+            remote(w, own_w, send.at[1], recv.at[1], peer),
+            remote(o, own_o, send.at[2], recv.at[2], peer),
+        ]
+        for copy in copies:
+            copy.start()
+        own_w[...] = w[...]
+        own_o[...] = o[...]
+        own_t[...] = t[...]
+        for copy in copies:
+            copy.wait()
+
+    return pl.pallas_call(
+        kernel,
+        out_shape=(
+            jax.ShapeDtypeStruct((2 * rows, qkv_cols), qkv_weight.dtype),
+            jax.ShapeDtypeStruct((head_rows, 2 * half), out_weight.dtype),
+            jax.ShapeDtypeStruct((2 * count, width), tokens.dtype),
+        ),
+        in_specs=[VMEM] * 3,
+        out_specs=(VMEM,) * 3,
+        scratch_shapes=[DMA((3,)), DMA((3,))],
+        compiler_params=params(1),
+    )(qkv_weight, out_weight, tokens)
+
+
+def gelu_parts(v):
+    root = 0.7978845608028654
+    t = jnp.tanh(root * (v + 0.044715 * v * v * v))
+    value = 0.5 * v * (1.0 + t)
+    slope = 0.5 * (1.0 + t) + 0.5 * v * (1.0 - t * t) * (root * (1.0 + 3 * 0.044715 * v * v))
+    return value, slope
+
+
+def expert_kernel(n_ex, n_col, cap, *refs):
+    (out_b, w_in, w_out, back, g_in, g_out, p_in, p_out, land, part, got, summed,
+     s_in, s_out, r_in, r_out, wsend, wrecv, xsend, xrecv, csend, crecv,
+     psend, precv, bsend, brecv, gsend, grecv) = refs
+    bf16, f32 = jnp.bfloat16, jnp.float32
+    ex, row, col = lax.axis_index("ex"), lax.axis_index("row"), lax.axis_index("col")
+    width = w_in.shape[0]
+    tokens = n_ex * n_col * cap
+    ex_peers, col_peers = others("ex"), others("col")
+    mate = {"row": 1 - row}
+    greet([{"ex": p} for p in ex_peers] + [{"col": p} for p in col_peers] + [mate])
+    first = [
+        remote(out_b.at[p], land.at[col, ex], xsend.at[k], xrecv.at[k], {"ex": p})
+        for k, p in enumerate(ex_peers)
+    ]
+    for copy in first:
+        copy.start()
+    weights = [
+        remote(w_in, p_in, wsend.at[0], wrecv.at[0], mate),
+        remote(w_out, p_out, wsend.at[1], wrecv.at[1], mate),
+    ]
+    land[col, ex] = out_b[ex]
+    spread = []
+
+    def forward(slot, index):
+        for k, p in enumerate(col_peers):
+            copy = remote(
+                land.at[col, slot], land.at[col, slot],
+                csend.at[index, k], crecv.at[index, k], {"col": p},
+            )
+            copy.start()
+            spread.append(copy)
+
+    forward(ex, 0)
+    for copy in weights:
+        copy.start()
+    for k, copy in enumerate(first):
+        copy.wait_recv()
+        forward(lax.rem(ex + n_ex - 1 - k, n_ex), 1 + k)
+    for copy in spread:
+        copy.wait_recv()
+    for copy in weights:
+        copy.wait()
+    x = land[:, :, :cap, :].reshape(tokens, width)
+    g = land[:, :, cap:, :].reshape(tokens, width)
+    y = jnp.zeros((tokens, width), f32)
+    d = jnp.zeros((tokens, width), f32)
+    kept = []
+    for wi, wo in ((w_in, w_out), (p_in, p_out)):
+        pre = jnp.dot(x, wi[...], preferred_element_type=f32)
+        value, slope = gelu_parts(pre)
+        hid = value.astype(bf16)
+        y = y + jnp.dot(hid, wo[...], preferred_element_type=f32)
+        d_hid = lax.dot_general(g, wo[...], INNER, preferred_element_type=f32)
+        d_pre = (d_hid * slope).astype(bf16)
+        d = d + lax.dot_general(d_pre, wi[...], INNER, preferred_element_type=f32)
+        kept.append((hid, d_pre))
+    part[:, :, :cap, :] = y.astype(bf16).reshape(n_col, n_ex, cap, width)
+    part[:, :, cap:, :] = d.astype(bf16).reshape(n_col, n_ex, cap, width)
+    sums = [
+        remote(part.at[p], got.at[k], psend.at[k], precv.at[k], {"col": p})
+        for k, p in enumerate(col_peers)
+    ]
+    for copy in sums:
+        copy.start()
+    s_in[...] = lax.dot_general(x, kept[1][1], OUTER, preferred_element_type=f32).astype(bf16)
+    s_out[...] = lax.dot_general(kept[1][0], g, OUTER, preferred_element_type=f32).astype(bf16)
+    grads = [
+        remote(s_in, r_in, gsend.at[0], grecv.at[0], mate),
+        remote(s_out, r_out, gsend.at[1], grecv.at[1], mate),
+    ]
+    for copy in grads:
+        copy.start()
+    for copy in sums:
+        copy.wait_recv()
+    total = part[col].astype(f32)
+    for k in range(n_col - 1):
+        total = total + got[k].astype(f32)
+    summed[...] = total.astype(bf16)
+    home = [
+        remote(summed.at[p], back.at[ex], bsend.at[k], brecv.at[k], {"ex": p})
+        for k, p in enumerate(ex_peers)
+    ]
+    for copy in home:
+        copy.start()
+    back[ex] = summed[ex]
+    g_in[...] = lax.dot_general(x, kept[0][1], OUTER, preferred_element_type=f32)
+    g_out[...] = lax.dot_general(kept[0][0], g, OUTER, preferred_element_type=f32)
+    for copy in grads:
+        copy.wait_recv()
+    g_in[...] += r_in[...].astype(f32)
+    g_out[...] += r_out[...].astype(f32)
+    for copy in home:
+        copy.wait()
+    for copy in first + spread + sums + grads:
+        copy.wait_send()
+
+
+def expert_block(outbound, w_in, w_out):
+    n_ex, twice, width = outbound.shape
+    n_col = lax.axis_size("col")
+    cap = twice // 2
+    bf16 = jnp.bfloat16
+    cols = w_in.shape[1]
+    return pl.pallas_call(
+        lambda *refs: expert_kernel(n_ex, n_col, cap, *refs),
+        out_shape=(
+            jax.ShapeDtypeStruct((n_ex, twice, width), bf16),
+            jax.ShapeDtypeStruct((width, cols), jnp.float32),
+            jax.ShapeDtypeStruct((cols, width), jnp.float32),
+        ),
+        in_specs=[VMEM] * 3,
+        out_specs=(VMEM,) * 3,
+        scratch_shapes=[
+            pltpu.VMEM((width, cols), bf16),
+            pltpu.VMEM((cols, width), bf16),
+            pltpu.VMEM((n_col, n_ex, twice, width), bf16),
+            pltpu.VMEM((n_col, n_ex, twice, width), bf16),
+            pltpu.VMEM((n_col - 1, n_ex, twice, width), bf16),
+            pltpu.VMEM((n_ex, twice, width), bf16),
+            pltpu.VMEM((width, cols), bf16),
+            pltpu.VMEM((cols, width), bf16),
+            pltpu.VMEM((width, cols), bf16),
+            pltpu.VMEM((cols, width), bf16),
+            DMA((2,)), DMA((2,)),
+            DMA((n_ex - 1,)), DMA((n_ex - 1,)),
+            DMA((n_ex, n_col - 1)), DMA((n_ex, n_col - 1)),
+            DMA((n_col - 1,)), DMA((n_col - 1,)),
+            DMA((n_ex - 1,)), DMA((n_ex - 1,)),
+            DMA((2,)), DMA((2,)),
+        ],
+        compiler_params=params(4),
+    )(outbound, w_in, w_out)
+
+
+def final_kernel(n_ex, *refs):
+    (qkv, out, small, qkv_o, out_o, small_o, ql, ol, qs, os_, qx, ox,
+     qf, of_, sl, sx, sc, sa, sb,
+     rsend, rrecv, esend, erecv, asend, arecv, csend, crecv) = refs
+    bf16, f32 = jnp.bfloat16, jnp.float32
+    ex, row, col = lax.axis_index("ex"), lax.axis_index("row"), lax.axis_index("col")
+    ex_peers, col_peers = others("ex"), others("col")
+    mate = {"row": 1 - row}
+    greet([{"ex": p} for p in ex_peers] + [{"col": p} for p in col_peers] + [mate])
+    waits = []
+    one = [
+        remote(small, sl, rsend.at[2], rrecv.at[2], mate),
+        remote(qkv.at[1 - row], ql, rsend.at[0], rrecv.at[0], mate),
+        remote(out.at[1 - row], ol, rsend.at[1], rrecv.at[1], mate),
+    ]
+    for copy in one:
+        copy.start()
+    one[0].wait_recv()
+    sa[...] = small[...] + sl[...]
+    small_ex = [
+        remote(sa, sx.at[k], esend.at[2, k], erecv.at[2, k], {"ex": p})
+        for k, p in enumerate(ex_peers)
+    ]
+    for copy in small_ex:
+        copy.start()
+    one[1].wait_recv()
+    qs[...] = (qkv[row].astype(f32) + ql[...].astype(f32)).astype(bf16).reshape(qs.shape)
+    q_ex = [
+        remote(qs.at[p], qx.at[k], esend.at[0, k], erecv.at[0, k], {"ex": p})
+        for k, p in enumerate(ex_peers)
+    ]
+    for copy in q_ex:
+        copy.start()
+    one[2].wait_recv()
+    os_[...] = (out[row].astype(f32) + ol[...].astype(f32)).astype(bf16).reshape(os_.shape)
+    o_ex = [
+        remote(os_.at[p], ox.at[k], esend.at[1, k], erecv.at[1, k], {"ex": p})
+        for k, p in enumerate(ex_peers)
+    ]
+    for copy in o_ex:
+        copy.start()
+    total = sa[...]
+    for k, copy in enumerate(small_ex):
+        copy.wait_recv()
+        total = total + sx[k]
+    sb[...] = total
+    small_col = [
+        remote(sb, sc.at[k], csend.at[k], crecv.at[k], {"col": p})
+        for k, p in enumerate(col_peers)
+    ]
+    for copy in small_col:
+        copy.start()
+    total = qs[ex].astype(f32)
+    for k, copy in enumerate(q_ex):
+        copy.wait_recv()
+        total = total + qx[k].astype(f32)
+    qf[ex] = total.astype(bf16)
+    gathers = [
+        remote(qf.at[ex], qf.at[ex], asend.at[0, k], arecv.at[0, k], {"ex": p})
+        for k, p in enumerate(ex_peers)
+    ]
+    for copy in gathers:
+        copy.start()
+    total = os_[ex].astype(f32)
+    for k, copy in enumerate(o_ex):
+        copy.wait_recv()
+        total = total + ox[k].astype(f32)
+    of_[ex] = total.astype(bf16)
+    more = [
+        remote(of_.at[ex], of_.at[ex], asend.at[1, k], arecv.at[1, k], {"ex": p})
+        for k, p in enumerate(ex_peers)
+    ]
+    for copy in more:
+        copy.start()
+    whole = sb[...]
+    for k, copy in enumerate(small_col):
+        copy.wait_recv()
+        whole = whole + sc[k]
+    spot = lax.broadcasted_iota(jnp.int32, whole.shape, 0)
+    small_o[...] = jnp.where(spot == 0, sb[...], whole)
+    for copy in gathers:
+        copy.wait_recv()
+    qkv_o[...] = qf[...].astype(f32).reshape(qkv_o.shape)
+    for copy in more:
+        copy.wait_recv()
+    out_o[...] = of_[...].astype(f32).reshape(out_o.shape)
+    for copy in one + small_ex + q_ex + o_ex + small_col + gathers + more:
+        copy.wait_send()
+
+
+def final_sums(qkv, out, small):
+    n_ex, n_col = lax.axis_size("ex"), lax.axis_size("col")
+    bf16, f32 = jnp.bfloat16, jnp.float32
+    _, qr, qc = qkv.shape
+    _, orr, oc = out.shape
+    return pl.pallas_call(
+        lambda *refs: final_kernel(n_ex, *refs),
+        out_shape=(
+            jax.ShapeDtypeStruct((qr, qc), f32),
+            jax.ShapeDtypeStruct((orr, oc), f32),
+            jax.ShapeDtypeStruct(small.shape, f32),
+        ),
+        in_specs=[VMEM] * 3,
+        out_specs=(VMEM,) * 3,
+        scratch_shapes=[
+            pltpu.VMEM((qr, qc), bf16),
+            pltpu.VMEM((orr, oc), bf16),
+            pltpu.VMEM((n_ex, qr // n_ex, qc), bf16),
+            pltpu.VMEM((n_ex, orr // n_ex, oc), bf16),
+            pltpu.VMEM((n_ex - 1, qr // n_ex, qc), bf16),
+            pltpu.VMEM((n_ex - 1, orr // n_ex, oc), bf16),
+            pltpu.VMEM((n_ex, qr // n_ex, qc), bf16),
+            pltpu.VMEM((n_ex, orr // n_ex, oc), bf16),
+            pltpu.VMEM(small.shape, f32),
+            pltpu.VMEM((n_ex - 1, *small.shape), f32),
+            pltpu.VMEM((n_col - 1, *small.shape), f32),
+            pltpu.VMEM(small.shape, f32),
+            pltpu.VMEM(small.shape, f32),
+            DMA((3,)), DMA((3,)),
+            DMA((3, n_ex - 1)), DMA((3, n_ex - 1)),
+            DMA((2, n_ex - 1)), DMA((2, n_ex - 1)),
+            DMA((n_col - 1,)), DMA((n_col - 1,)),
+        ],
+        compiler_params=params(8),
+    )(qkv, out, small)
+
+
+def expert_exchange(outbound, w_in, w_out):
+    n_ex, twice, width = outbound.shape
+    cap = twice // 2
+    arrived = lax.all_to_all(outbound, "ex", split_axis=0, concat_axis=0, tiled=True)
+    arrived = lax.all_gather(arrived, "col", axis=0, tiled=True)
+    x = arrived[:, :cap].reshape(-1, width)
+    g = arrived[:, cap:].reshape(-1, width)
+    inner = lax.all_gather(w_in, "row", axis=1, tiled=True)
+    outer = lax.all_gather(w_out, "row", axis=0, tiled=True)
+    pre = jnp.dot(x, inner, preferred_element_type=jnp.float32)
+    value, slope = gelu_parts(pre)
+    hid = value.astype(jnp.bfloat16)
+    y = jnp.dot(hid, outer, preferred_element_type=jnp.float32)
+    d_hid = lax.dot_general(g, outer, INNER, preferred_element_type=jnp.float32)
+    d_pre = (d_hid * slope).astype(jnp.bfloat16)
+    d = lax.dot_general(d_pre, inner, INNER, preferred_element_type=jnp.float32)
+    g_in = lax.dot_general(x, d_pre, OUTER, preferred_element_type=jnp.float32)
+    g_out = lax.dot_general(hid, g, OUTER, preferred_element_type=jnp.float32)
+    both = jnp.concatenate([y.reshape(-1, cap, width), d.reshape(-1, cap, width)], axis=1)
+    both = lax.psum_scatter(both, "col", scatter_dimension=0, tiled=True).astype(jnp.bfloat16)
+    back = lax.all_to_all(both, "ex", split_axis=0, concat_axis=0, tiled=True)
+    g_in = lax.psum_scatter(g_in, "row", scatter_dimension=1, tiled=True)
+    g_out = lax.psum_scatter(g_out, "row", scatter_dimension=0, tiled=True)
+    return back, g_in, g_out
 
 
 def on_device(
@@ -63,11 +498,8 @@
     heads = out_weight.shape[0] // HDIM
     buckets = bias_table.shape[0]
     scale = HDIM ** (-0.5)
-    qkv_rows, out_rows, group_tokens = (
-        lax.all_gather(qkv_weight, "row", axis=0, tiled=True),
-        lax.all_gather(out_weight, "row", axis=1, tiled=True),
-        lax.all_gather(tokens, "row", axis=0, tiled=True),
-    )
+    direct = cap % 16 == 0
+    qkv_rows, out_rows, group_tokens = gather_row(qkv_weight, out_weight, tokens)
     group = group_tokens.shape[0]
     local_offset = my_row * tokens_per_device
     quarter_offset = my_col * dispatch_mask
@@ -115,11 +547,12 @@
 
     mixed, log_total = lax.map(attend, (queries, keys, values, bias_lines))
     attn = mixed.transpose(1, 0, 2).reshape(tokens_per_device, heads * HDIM).astype(jnp.bfloat16)
-    branch = lax.psum_scatter(
-        jnp.dot(attn, out_rows, preferred_element_type=jnp.float32),
+    branch = scatter_sum(
+        jnp.dot(attn, out_rows, preferred_element_type=jnp.float32)
+        .astype(jnp.bfloat16)
+        .reshape(n_col, dispatch_mask, width),
         "col",
-        scatter_dimension=0,
-        tiled=True,
+        2,
     )
     hidden_state = (
         lax.dynamic_slice_in_dim(tokens, quarter_offset, dispatch_mask, 0).astype(jnp.float32)
@@ -145,57 +578,28 @@
     )
     scaled_grad = (gate * upstream).astype(jnp.bfloat16)
     place = route_here * cap + slot_here
-    outbound = (
-        jnp.zeros((experts * cap, width), jnp.bfloat16)
-        .at[place]
-        .set(second_normed_input)
-        .reshape(experts, cap, width)
-    )
-    outbound_grad = (
-        jnp.zeros((experts * cap, width), jnp.bfloat16)
-        .at[place]
-        .set(scaled_grad)
-        .reshape(experts, cap, width)
-    )
-    arrived, arrived_grad = (
-        lax.all_to_all(outbound, "ex", split_axis=0, concat_axis=0, tiled=True),
-        lax.all_to_all(outbound_grad, "ex", split_axis=0, concat_axis=0, tiled=True),
-    )
-    arrived = arrived.reshape(experts * cap, width)
-    arrived_grad = arrived_grad.reshape(experts * cap, width)
-    inner, outer = (
-        lax.all_gather(expert_in[0], ("row", "col"), axis=1, tiled=True),
-        lax.all_gather(expert_out[0], ("row", "col"), axis=0, tiled=True),
-    )
-    pre = jnp.dot(arrived, inner, preferred_element_type=jnp.float32)
-    activated, pull = jax.vjp(gelu_tanh, pre)
-    hidden = activated.astype(jnp.bfloat16)
-    expert_y = jnp.dot(hidden, outer, preferred_element_type=jnp.float32).astype(jnp.bfloat16)
-    hidden_grad = lax.dot_general(arrived_grad, outer, INNER, preferred_element_type=jnp.float32)
-    pre_grad = pull(hidden_grad)[0].astype(jnp.bfloat16)
-    entry_grad = lax.dot_general(pre_grad, inner, INNER, preferred_element_type=jnp.float32).astype(
+    put = (jnp.arange(experts * cap, dtype=jnp.int32)[:, None] == place[None, :]).astype(
         jnp.bfloat16
     )
-    inner_full = lax.dot_general(arrived, pre_grad, OUTER, preferred_element_type=jnp.float32)
-    outer_full = lax.dot_general(hidden, arrived_grad, OUTER, preferred_element_type=jnp.float32)
-    inner_grad, outer_grad = (
-        lax.psum_scatter(
-            inner_full.astype(jnp.bfloat16), ("row", "col"), scatter_dimension=1, tiled=True
-        ).astype(jnp.float32),
-        lax.psum_scatter(
-            outer_full.astype(jnp.bfloat16), ("row", "col"), scatter_dimension=0, tiled=True
-        ).astype(jnp.float32),
-    )
-    returned, returned_grad = (
-        lax.all_to_all(
-            expert_y.reshape(experts, cap, width), "ex", split_axis=0, concat_axis=0, tiled=True
-        ),
-        lax.all_to_all(
-            entry_grad.reshape(experts, cap, width), "ex", split_axis=0, concat_axis=0, tiled=True
-        ),
-    )
-    expert_back_rows = returned.reshape(experts * cap, width)[place].astype(jnp.float32)
-    entry_back = returned_grad.reshape(experts * cap, width)[place].astype(jnp.float32)
+    outbound = jnp.concatenate(
+        [
+            jnp.dot(put, rows, preferred_element_type=jnp.float32)
+            .astype(jnp.bfloat16)
+            .reshape(experts, cap, width)
+            for rows in (second_normed_input, scaled_grad)
+        ],
+        axis=1,
+    )
+    if direct:
+        back, inner_grad, outer_grad = expert_block(outbound, expert_in[0], expert_out[0])
+    else:
+        back, inner_grad, outer_grad = expert_exchange(outbound, expert_in[0], expert_out[0])
+    expert_back_rows, entry_back = (
+        lax.dot_general(
+            put, rows.reshape(experts * cap, width), OUTER, preferred_element_type=jnp.float32
+        )
+        for rows in (back[:, :cap], back[:, cap:])
+    )
     output = hidden_state + gate * expert_back_rows
     gate_grad = jnp.sum(upstream * expert_back_rows, axis=1, keepdims=True)
     logit_grad = gates * (picks * gate_grad - gate * gate_grad)
@@ -210,7 +614,9 @@
         - second_unit_input
         * jnp.mean(second_scaled_input * second_unit_input, axis=1, keepdims=True)
     )
-    branch_all = lax.all_gather(state_grad.astype(jnp.bfloat16), "col", axis=0, tiled=True)
+    branch_all = gather_blocks(state_grad.astype(jnp.bfloat16), "col", 5).reshape(
+        tokens_per_device, width
+    )
     out_full = lax.dot_general(attn, branch_all, OUTER, preferred_element_type=jnp.float32)
     attn_grad = lax.dot_general(
         branch_all, out_rows, INNER, preferred_element_type=jnp.float32
@@ -241,16 +647,10 @@
     query_grads, key_grads, value_grads, diagonals = lax.map(
         attend_back, (queries, keys, values, bias_lines, log_total, attn_grad)
     )
-    key_cols = key_grads.transpose(1, 0, 2).reshape(group, heads * HDIM)
-    value_cols = value_grads.transpose(1, 0, 2).reshape(group, heads * HDIM)
-    key_own, value_own = (
-        lax.psum_scatter(
-            key_cols.astype(jnp.bfloat16), "row", scatter_dimension=0, tiled=True
-        ).astype(jnp.float32),
-        lax.psum_scatter(
-            value_cols.astype(jnp.bfloat16), "row", scatter_dimension=0, tiled=True
-        ).astype(jnp.float32),
-    )
+    pairs = jnp.concatenate([key_grads, value_grads], axis=0).astype(jnp.bfloat16)
+    pairs = pairs.transpose(1, 0, 2).reshape(2, tokens_per_device, 2 * heads * HDIM)
+    own_pairs = scatter_sum(pairs, "row", 6).reshape(tokens_per_device, 2, heads, HDIM)
+    key_own, value_own = own_pairs[:, 0], own_pairs[:, 1]
     stacked = jnp.stack(
         [
             query_grads.transpose(1, 0, 2),
@@ -270,22 +670,8 @@
     )
     first_norm_slice = jnp.sum(first_normed_slice * local_unit_input, axis=0)
     table_part = jnp.dot(table_rows.T, diagonals.T, precision=HIGH)
-    norm1_tiles = jnp.broadcast_to(first_norm_slice[None], (n_col, width))
-    norm2_tiles = jnp.broadcast_to(second_norm_slice[None], (n_col, width))
-    router_tiles = jnp.broadcast_to(router_part[None], (n_col, width, experts))
-    xn_one_grad, norm1_cols, norm2_cols, router_cols = (
-        lax.psum_scatter(
-            first_normed_slice.astype(jnp.bfloat16), "col", scatter_dimension=0, tiled=True
-        ).astype(jnp.float32),
-        lax.psum_scatter(
-            norm1_tiles.astype(jnp.bfloat16), "col", scatter_dimension=0, tiled=True
-        ).astype(jnp.float32),
-        lax.psum_scatter(
-            norm2_tiles.astype(jnp.bfloat16), "col", scatter_dimension=0, tiled=True
-        ).astype(jnp.float32),
-        lax.psum_scatter(
-            router_tiles.astype(jnp.bfloat16), "col", scatter_dimension=0, tiled=True
-        ).astype(jnp.float32),
+    xn_one_grad = scatter_sum(
+        first_normed_slice.astype(jnp.bfloat16).reshape(n_col, dispatch_mask, width), "col", 7
     )
     quarter_unit_input = lax.dynamic_slice_in_dim(
         local_unit_input, quarter_offset, dispatch_mask, 0
@@ -299,13 +685,27 @@
         - quarter_unit_input
         * jnp.mean(first_scaled_input * quarter_unit_input, axis=1, keepdims=True)
     )
-    qkv_sum, out_sum, table_grad, norm1_grad, norm2_grad, router_grad = lax.psum(
-        (qkv_full, out_full, table_part, norm1_cols[0], norm2_cols[0], router_cols[0]),
-        ("ex", "row"),
-    )
     half = width // lax.axis_size("row")
-    qkv_grad = lax.dynamic_slice_in_dim(qkv_sum, my_row * half, half, 0)
-    out_grad = lax.dynamic_slice_in_dim(out_sum, my_row * half, half, 1)
+    if direct:
+        flat = jnp.pad(table_part.reshape(1, -1), ((0, 0), (0, width - buckets * heads)))
+        small = jnp.concatenate(
+            [flat, first_norm_slice[None], second_norm_slice[None], router_part.T], axis=0
+        )
+        small = jnp.pad(small, ((0, -small.shape[0] % 8), (0, 0)))
+        qkv_grad, out_grad, small = final_sums(
+            qkv_full.astype(jnp.bfloat16).reshape(2, half, -1),
+            out_full.astype(jnp.bfloat16).reshape(-1, 2, half).transpose(1, 0, 2),
+            small,
+        )
+        table_grad = small[0, : buckets * heads].reshape(buckets, heads)
+        norm1_grad, norm2_grad, router_grad = small[1], small[2], small[3 : 3 + experts].T
+    else:
+        qkv_sum, out_sum, table_grad = lax.psum((qkv_full, out_full, table_part), ("ex", "row"))
+        norm1_grad, norm2_grad, router_grad = lax.psum(
+            (first_norm_slice, second_norm_slice, router_part), ("ex", "row", "col")
+        )
+        qkv_grad = lax.dynamic_slice_in_dim(qkv_sum, my_row * half, half, 0)
+        out_grad = lax.dynamic_slice_in_dim(out_sum, my_row * half, half, 1)
     return (
         output,
         input_grad,

time: 424 us -> 144 us (0.34)
  waiting for transfers between devices: 227 us -> 0 us
  Pallas kernels: 0 us -> 89.3 us
  blocking collectives: 60.7 us -> 0 us
  matrix products: 48.8 us -> 15 us
  starting transfers between devices: 16.2 us -> 0 us
  between operations: 16.2 us -> 1.41 us
  local copies, waits for them, and re-layouts: 37.7 us -> 29.4 us
  other arithmetic: 15.4 us -> 7.78 us
    reduce_scatter x3 -> x0, waiting for transfers between devices: 99 us -> none  [the longest x1 54.9 us: on_device(): lax.psum_scatter(outer_full.astype(jnp.bfloat16), ('row', 'col'), scatter...]
    pallas_call x0 -> x7, Pallas kernels: none -> 89.3 us  [the longest x1 33.8 us: final_sums(): pl.pallas_call(lambda *refs: final_kernel(n_ex, *refs), out_shape=(jax.Sh...]
    unnamed x12 -> x0, waiting for transfers between devices: 67.8 us -> none
    psum x1 -> x0, waiting for transfers between devices: 27.5 us -> none  [on_device(): lax.psum((qkv_full, out_full, table_part, norm1_cols[0], norm2_cols[0], r...]
    psum x1 -> x0, blocking collectives: 27.2 us -> none  [on_device(): lax.psum((qkv_full, out_full, table_part, norm1_cols[0], norm2_cols[0], r...]
    dot_general x6 -> x4, matrix products: 20.8 us -> 1.84 us  [the longest x2 1.46 us: on_device(): lax.dot_general(put, rows.reshape(experts * cap, width), OUTER, preferred...]
    all_gather x2 -> x0, waiting for transfers between devices: 18.8 us -> none  [the longest x1 18.8 us: on_device(): lax.all_gather(expert_out[0], ('row', 'col'), axis=0, tiled=True)]
    unnamed x1 -> x0, blocking collectives: 16.8 us -> none
  transfers between devices with their start and end apart: 13 -> 0, of which waited for: 11 -> 0; matrix products, arithmetic and copies ran while one was open for 10% -> 0% of each run, Pallas kernels for 0% -> 0%
where the time goes in v1:
time: 144 us
  Pallas kernels  89.3 us (62%)
  local copies, waits for them, and re-layouts  29.4 us (20%)
  matrix products  15 us (10%)
  other arithmetic  7.78 us (5%)
    pallas_call x1, Pallas kernels, final_sums(): pl.pallas_call(lambda *refs: final_kernel(n_ex, *refs), out_shape=(jax.Sh...  33.8 us
    pallas_call x1, Pallas kernels, expert_block(): pl.pallas_call(lambda *refs: expert_kernel(n_ex, n_col, cap, *refs), out_...  30.5 us
    pallas_call x3, Pallas kernels, scatter_sum(): pl.pallas_call(kernel, out_shape=jax.ShapeDtypeStruct(blocks.shape[1:], j...  16.7 us
    unnamed x80, local copies, waits for them, and re-layouts  9.17 us
    pallas_call x1, Pallas kernels, gather_blocks(): pl.pallas_call(kernel, out_shape=jax.ShapeDtypeStruct((size, *block.shape...  5.68 us
    dot_general x3, matrix products, attend_back(): jnp.einsum('qd,kd->qk', grad, value, preferred_element_type=jnp.float32)  3.77 us

profile of v1, /device:TPU:0, one launch (start us, length us, event | category | flops | bytes accessed | tf_op | source)
XLA Modules:
  0.0 143.6 jit_solution(11313635456177656123)
XLA Ops:
  0.7 0.9 reduce-window.8
  1.6 0.8 dynamic-slice_add_fusion
  2.5 1.0 convolution_bitcast_fusion.2
  3.6 1.3 copy.44.w
  4.9 2.7 %shard_map.204 = (bf16[768,576]{1,0:T(8,128)(2,1)S(1)}, bf16[192,768]{1,0:T(8,128)(2,1)S(1)}, bf16[384,768]{1,0:T(8,128)(2,1)S(1)}) custom-call(bf16[384,576]{1,0:T(8,128)(2,1)S(1)} %copy.44.w, bf16[192,384]{1,0:T(8,128)(2,1)S(1)} %copy-done.9, bf16[192,768]{1,0:T(8,128)(2,1)S(1)} %copy-done.7), custom_call_target="tpu_custom_call" | custom-call | tf_op jit(solution)/shard_map/pallas_call | solution.py:166
  7.8 0.7 dynamic-slice.4
  8.5 1.2 convert_multiply_fusion
  9.7 0.7 convolution_convert_fusion.1
  11.0 7.0 %while.32 = (s32[]{:T(128)}, bf16[3,192,64]{1,2,0:T(8,128)(2,1)S(1)}, f32[3,192,1]{1,2,0:T(1,128)}, bf16[3,192,64]{2,1,0:T(8,128)(2,1)S(1)}, bf16[3,384,64]{2,1,...) while((s32[]{:T(128)}, ...), condition=%wide.region_6.7_spmd.clone, body=%wide.region_3.6_spmd.clone.sunk | while | flops 19611456 | bytes 3717993 | solution.py:548
  11.5 0.5 reshape.273
  12.8 0.6 constant_dynamic-update-slice_fusion.2
  15.2 0.6 constant_dynamic-update-slice_fusion.2
  16.2 0.5 reshape.273
  17.5 0.6 constant_dynamic-update-slice_fusion.2
  18.4 8.4 %shard_map.205 = f32[48,768]{1,0:T(8,128)S(1)} custom-call(bf16[4,48,768]{2,1,0:T(8,128)(2,1)S(1)} %bitcast.177), custom_call_target="tpu_custom_call" | custom-call | tf_op jit(solution)/shard_map/pallas_call | solution.py:127
  27.7 30.5 %shard_map.206 = (bf16[4,32,768]{2,1,0:T(8,128)(2,1)S(1)}, f32[768,384]{1,0:T(8,128)S(1)}, f32[384,768]{1,0:T(8,128)S(1)}) custom-call(bf16[4,32,768]{2,1,0:T(8,128)(2,1)S(1)} %pad_maximum_fusion.1.refs_0_, bf16[768,384]{1,0:T(8,128)(2,1)S(1)} %bitcast.178, bf16[384,768]{1,0:T(8,128)(2,1)S(1)} %bitcast.179), custom_call_target="tpu_custom_call" | custom-call | tf_op jit(solution)/shard_map/pallas_call | solution.py:292
  58.2 1.1 fusion.52
  59.3 0.8 fusion.82
  60.7 0.6 broadcast_in_dim.88
  61.5 5.7 %shard_map.207 = bf16[4,48,768]{2,1,0:T(8,128)(2,1)S(1)} custom-call(bf16[48,768]{1,0:T(8,128)(2,1)S(1)} %fusion.94.x), custom_call_target="tpu_custom_call" | custom-call | tf_op jit(solution)/shard_map/pallas_call | solution.py:96
  67.9 0.7 broadcast.172
  68.5 17.2 %while.33 = (s32[]{:T(128)}, bf16[3,192,64]{1,2,0:T(8,128)(2,1)}, bf16[3,384,64]{1,2,0:T(8,128)(2,1)}, bf16[3,384,64]{1,2,0:T(8,128)(2,1)}, f32[3,575]{1,0:T(4,1...) while((s32[]{:T(128)}, bf16[3,192,64]{1,2,0:T(8,128)(2,1)}, ...), condition=%wide.region_16.17_spmd.clone, body=%wide.region_13.16_spmd.clone.sunk | while | flops 48253824 | bytes 11297815 | solution.py:647
  68.5 0.7 constant_dynamic-slice_fusion.2
  70.9 1.3 multiply_reduce_fusion.7
  73.1 0.5 reshape.276
  74.3 0.7 constant_dynamic-slice_fusion.2
  76.6 1.3 multiply_reduce_fusion.7
  78.9 0.5 reshape.276
  80.1 0.7 constant_dynamic-slice_fusion.2
  82.4 1.3 multiply_reduce_fusion.7
  84.6 0.5 reshape.276
  86.4 1.0 maximum_bitcast_fusion
  87.6 0.8 copy.47.x
  88.4 1.5 %shard_map.208 = f32[192,384]{1,0:T(8,128)S(1)} custom-call(bf16[2,192,384]{2,1,0:T(8,128)(2,1)S(1)} %copy.47.x), custom_call_target="tpu_custom_call" | custom-call | tf_op jit(solution)/shard_map/pallas_call | solution.py:127
  90.2 0.9 copy-done.4
  91.5 0.5 multiply_reduce_fusion.1
  92.5 6.8 %shard_map.209 = f32[48,768]{1,0:T(8,128)S(1)} custom-call(bf16[4,48,768]{2,1,0:T(8,128)(2,1)S(1)} %bitcast.173), custom_call_target="tpu_custom_call" | custom-call | tf_op jit(solution)/shard_map/pallas_call | solution.py:127
  99.6 1.7 %multiply_add_fusion = (f32[48,768]{1,0:T(8,128)}, f32[48,768]{1,0:T(8,128)}) fusion(f32[48,768]{1,0:T(8,128)S(1)} %shard_map.209, f32[384,768]{1,0:T(8,128)S(1)} %copy-done.12, s32[]{:T(128)S(6)} %dynamic_slice.92, f32[48]{0:T(128)S(1)} %broadcast_multiply_fusion, f32[768]{0:T(1024)S(1)} %copy-done.33, f32[48]{0:T(128)S(1)} %copy-done.43, ...), kind=kLoop, calls=%fused_computation.92 | loop fusion | flops 516096 | bytes 1113032 | tf_op jit(solution)/shard_map/add | solution.py:683
  101.4 0.6 copy.50
  102.0 33.8 %shard_map.210 = (f32[384,576]{1,0:T(8,128)S(1)}, f32[192,384]{1,0:T(8,128)S(1)}, f32[8,768]{1,0:T(8,128)S(1)}) custom-call(bf16[2,384,576]{2,1,0:T(8,128)(2,1)S(1)} %bitcast.170, bf16[2,192,384]{2,1,0:T(8,128)(2,1)S(1)} %bitcast.174, f32[8,768]{1,0:T(8,128)S(1)} %pad.25.refs_2_), custom_call_target="tpu_custom_call" | custom-call | tf_op jit(solution)/shard_map/pallas_call | solution.py:418
  135.9 0.7 copy-done.8
  136.6 1.2 copy.53
  137.8 0.6 slice_reduce_fusion
  138.5 0.6 slice_bitcast_fusion.4
  139.2 0.7 copy.54
  139.8 1.7 %copy.94 = f32[192,384]{1,0:T(8,128)} copy(f32[192,384]{1,0:T(8,128)} %copy-done.8) | data formatting | bytes 589824
  141.5 1.0 copy.95
  142.5 1.0 copy.96
  (236 shorter events, 19.4 us)
Async XLA Ops:
  0.6 26.4 %copy-start = (bf16[768,4]{0,1:T(4,128)(2,1)S(1)}, bf16[768,4]{0,1:T(4,128)(2,1)}, u32[]{:S(2)}) copy-start(bf16[768,4]{0,1:T(4,128)(2,1)} %param.23) | copy-start | bytes 18436
  0.7 4.2 %copy-start.7 = (bf16[192,768]{1,0:T(8,128)(2,1)S(1)}, bf16[192,768]{1,0:T(8,128)(2,1)}, u32[]{:S(2)}) copy-start(bf16[192,768]{1,0:T(8,128)(2,1)} %t.1) | copy-start | bytes 884740
  0.7 4.2 %copy-start.9 = (bf16[192,384]{1,0:T(8,128)(2,1)S(1)}, bf16[192,384]{1,0:T(8,128)(2,1)}, u32[]{:S(2)}) copy-start(bf16[192,384]{1,0:T(8,128)(2,1)} %o.1) | copy-start | bytes 442372
  2.5 5.0 %copy-start.39 = (s32[575]{0:T(1024)}, s32[575]{0:T(1024)S(1)}, u32[]{:S(2)}) copy-start(s32[575]{0:T(1024)S(1)} %fusion.68) | copy-start | bytes 6904
  3.6 4.9 %copy-start.32 = (f32[768]{0:T(1024)S(1)}, f32[768]{0:T(1024)}, u32[]{:S(2)}) copy-start(f32[768]{0:T(1024)} %param.21) | copy-start | bytes 9220
  7.5 2.1 %copy-start.3 = (bf16[768,576]{1,0:T(8,128)(2,1)}, bf16[768,576]{1,0:T(8,128)(2,1)S(1)}, u32[]{:S(2)}) copy-start(bf16[768,576]{1,0:T(8,128)(2,1)S(1)} %get-tuple-element.215) | copy-start | bytes 2654212
  18.1 9.5 %copy-start.13 = (bf16[3,384,64]{2,1,0:T(8,128)(2,1)}, bf16[3,384,64]{2,1,0:T(8,128)(2,1)S(1)}, u32[]{:S(2)}) copy-start(bf16[3,384,64]{2,1,0:T(8,128)(2,1)S(1)} %get-tuple-element.633) | copy-start | bytes 442372
  18.1 8.8 %copy-start.27 = (f32[768]{0:T(1024)S(1)}, f32[768]{0:T(1024)}, u32[]{:S(2)}) copy-start(f32[768]{0:T(1024)} %param.22) | copy-start | bytes 9220
  18.1 9.1 %copy-start.22 = (bf16[192,768]{1,0:T(8,128)(2,1)S(1)}, bf16[192,768]{1,0:T(8,128)(2,1)}, u32[]{:S(2)}) copy-start(bf16[192,768]{1,0:T(8,128)(2,1)} %param.29) | copy-start | bytes 884740
  18.1 9.6 %copy-start.5 = (bf16[1,768,384]{2,1,0:T(8,128)(2,1)S(1)}, bf16[1,768,384]{2,1,0:T(8,128)(2,1)}, u32[]{:S(2)}) copy-start(bf16[1,768,384]{2,1,0:T(8,128)(2,1)} %param.24) | copy-start | bytes 1769476
  18.1 9.6 %copy-start.6 = (bf16[1,384,768]{2,1,0:T(8,128)(2,1)S(1)}, bf16[1,384,768]{2,1,0:T(8,128)(2,1)}, u32[]{:S(2)}) copy-start(bf16[1,384,768]{2,1,0:T(8,128)(2,1)} %param.25) | copy-start | bytes 1769476
  26.9 34.4 %copy-start.10 = (f32[48,768]{1,0:T(8,128)}, f32[48,768]{1,0:T(8,128)S(1)}, u32[]{:S(2)}) copy-start(f32[48,768]{1,0:T(8,128)S(1)} %get-tuple-element.362) | copy-start | bytes 442372
  26.9 34.4 %copy-start.35 = (f32[48]{0:T(128)}, f32[48]{0:T(128)S(1)}, u32[]{:S(2)}) copy-start(f32[48]{0:T(128)S(1)} %add_rsqrt_fusion.1) | copy-start | bytes 580
  27.2 32.1 %copy-start.37 = (f32[48]{0:T(128)}, f32[48]{0:T(128)S(1)}, u32[]{:S(2)}) copy-start(f32[48]{0:T(128)S(1)} %get-tuple-element.359) | copy-start | bytes 580
  58.1 9.0 %copy-start.1 = (f32[768,384]{1,0:T(8,128)}, f32[768,384]{1,0:T(8,128)S(1)}, u32[]{:S(2)}) copy-start(f32[768,384]{1,0:T(8,128)S(1)} %get-tuple-element.227) | copy-start | bytes 3538948
  61.4 6.4 %copy-start.41 = (f32[48]{0:T(128)}, f32[48]{0:T(128)S(1)}, u32[]{:S(2)}) copy-start(f32[48]{0:T(128)S(1)} %broadcast_multiply_fusion.1) | copy-start | bytes 580
  67.2 1.4 copy-start.44
  68.5 17.3 %copy-start.40 = (s32[575]{0:T(1024)S(1)}, s32[575]{0:T(1024)}, u32[]{:S(2)}) copy-start(s32[575]{0:T(1024)} %copy-done.39) | copy-start | bytes 6904
  70.2 2.0 %copy-start.19 = (bf16[3,192,64]{1,2,0:T(8,128)(2,1)S(1)}, bf16[3,192,64]{1,2,0:T(8,128)(2,1)}, u32[]{:S(2)}) copy-start(bf16[3,192,64]{1,2,0:T(8,128)(2,1)} %get-tuple-element.578) | copy-start | bytes 221188 | tf_op jit(solution)/shard_map/while
  70.6 1.8 %copy-start.25 = (bf16[3,384,64]{1,2,0:T(8,128)(2,1)S(1)}, bf16[3,384,64]{1,2,0:T(8,128)(2,1)}, u32[]{:S(2)}) copy-start(bf16[3,384,64]{1,2,0:T(8,128)(2,1)} %get-tuple-element.579) | copy-start | bytes 442372 | tf_op jit(solution)/shard_map/while
  70.8 1.3 copy-start.24
  72.7 1.5 %copy-start.26 = (bf16[3,384,64]{1,2,0:T(8,128)(2,1)}, bf16[3,384,64]{1,2,0:T(8,128)(2,1)S(1)}, u32[]{:S(2)}) copy-start(bf16[3,384,64]{1,2,0:T(8,128)(2,1)S(1)} %fusion.151) | copy-start | bytes 442372 | tf_op jit(solution)/shard_map/while
  76.0 2.0 %copy-start.19 = (bf16[3,192,64]{1,2,0:T(8,128)(2,1)S(1)}, bf16[3,192,64]{1,2,0:T(8,128)(2,1)}, u32[]{:S(2)}) copy-start(bf16[3,192,64]{1,2,0:T(8,128)(2,1)} %get-tuple-element.578) | copy-start | bytes 221188 | tf_op jit(solution)/shard_map/while
  76.4 1.8 %copy-start.25 = (bf16[3,384,64]{1,2,0:T(8,128)(2,1)S(1)}, bf16[3,384,64]{1,2,0:T(8,128)(2,1)}, u32[]{:S(2)}) copy-start(bf16[3,384,64]{1,2,0:T(8,128)(2,1)} %get-tuple-element.579) | copy-start | bytes 442372 | tf_op jit(solution)/shard_map/while
  76.6 1.3 copy-start.24
  78.4 1.5 %copy-start.26 = (bf16[3,384,64]{1,2,0:T(8,128)(2,1)}, bf16[3,384,64]{1,2,0:T(8,128)(2,1)S(1)}, u32[]{:S(2)}) copy-start(bf16[3,384,64]{1,2,0:T(8,128)(2,1)S(1)} %fusion.151) | copy-start | bytes 442372 | tf_op jit(solution)/shard_map/while
  78.9 1.2 copy-start.30
  81.7 2.0 %copy-start.19 = (bf16[3,192,64]{1,2,0:T(8,128)(2,1)S(1)}, bf16[3,192,64]{1,2,0:T(8,128)(2,1)}, u32[]{:S(2)}) copy-start(bf16[3,192,64]{1,2,0:T(8,128)(2,1)} %get-tuple-element.578) | copy-start | bytes 221188 | tf_op jit(solution)/shard_map/while
  82.1 1.8 %copy-start.25 = (bf16[3,384,64]{1,2,0:T(8,128)(2,1)S(1)}, bf16[3,384,64]{1,2,0:T(8,128)(2,1)}, u32[]{:S(2)}) copy-start(bf16[3,384,64]{1,2,0:T(8,128)(2,1)} %get-tuple-element.579) | copy-start | bytes 442372 | tf_op jit(solution)/shard_map/while
  82.3 1.3 copy-start.24
  84.2 1.5 %copy-start.26 = (bf16[3,384,64]{1,2,0:T(8,128)(2,1)}, bf16[3,384,64]{1,2,0:T(8,128)(2,1)S(1)}, u32[]{:S(2)}) copy-start(bf16[3,384,64]{1,2,0:T(8,128)(2,1)S(1)} %fusion.151) | copy-start | bytes 442372 | tf_op jit(solution)/shard_map/while
  84.6 1.2 copy-start.30
  87.6 2.5 %copy-start.21 = (bf16[3,192,64]{1,2,0:T(8,128)(2,1)S(1)}, bf16[3,192,64]{1,2,0:T(8,128)(2,1)}, u32[]{:S(2)}) copy-start(bf16[3,192,64]{1,2,0:T(8,128)(2,1)} %get-tuple-element.220) | copy-start | bytes 221188
  89.9 1.2 copy-start.4
  90.0 1.4 copy-start.12
  90.2 1.8 %copy-start.17 = (bf16[384,768]{1,0:T(8,128)(2,1)S(1)}, bf16[384,768]{1,0:T(8,128)(2,1)}, u32[]{:S(2)}) copy-start(bf16[384,768]{1,0:T(8,128)(2,1)} %copy-done.16) | copy-start | bytes 1769476
  92.0 7.4 %copy-start.33 = (f32[768]{0:T(1024)S(1)}, f32[768]{0:T(1024)}, u32[]{:S(2)}) copy-start(f32[768]{0:T(1024)} %param.21) | copy-start | bytes 9220
  92.0 7.5 %copy-start.11 = (f32[48,768]{1,0:T(8,128)S(1)}, f32[48,768]{1,0:T(8,128)}, u32[]{:S(2)}) copy-start(f32[48,768]{1,0:T(8,128)} %copy-done.10) | copy-start | bytes 442372
  92.0 7.5 %copy-start.15 = (f32[48,768]{1,0:T(8,128)S(1)}, f32[48,768]{1,0:T(8,128)}, u32[]{:S(2)}) copy-start(f32[48,768]{1,0:T(8,128)} %copy-done.14) | copy-start | bytes 442372
  92.0 7.5 %copy-start.18 = (f32[48,768]{1,0:T(8,128)S(1)}, f32[48,768]{1,0:T(8,128)}, u32[]{:S(2)}) copy-start(f32[48,768]{1,0:T(8,128)} %get-tuple-element.385) | copy-start | bytes 442372
  92.0 7.5 %copy-start.28 = (f32[768]{0:T(1024)S(1)}, f32[768]{0:T(1024)}, u32[]{:S(2)}) copy-start(f32[768]{0:T(1024)} %param.22) | copy-start | bytes 9220
  92.1 7.5 %copy-start.36 = (f32[48]{0:T(128)S(1)}, f32[48]{0:T(128)}, u32[]{:S(2)}) copy-start(f32[48]{0:T(128)} %copy-done.35) | copy-start | bytes 580
  92.1 7.5 %copy-start.38 = (f32[48]{0:T(128)S(1)}, f32[48]{0:T(128)}, u32[]{:S(2)}) copy-start(f32[48]{0:T(128)} %copy-done.37) | copy-start | bytes 580
  92.1 7.5 %copy-start.42 = (f32[48]{0:T(128)S(1)}, f32[48]{0:T(128)}, u32[]{:S(2)}) copy-start(f32[48]{0:T(128)} %copy-done.41) | copy-start | bytes 580
  92.1 7.5 %copy-start.43 = (f32[48]{0:T(128)S(1)}, f32[48]{0:T(128)}, u32[]{:S(2)}) copy-start(f32[48]{0:T(128)} %dynamic-slice.4) | copy-start | bytes 580
  92.5 8.9 %copy-start.31 = (f32[4,768]{1,0:T(4,128)S(1)}, f32[4,768]{1,0:T(4,128)}, u32[]{:S(2)}) copy-start(f32[4,768]{1,0:T(4,128)} %fusion.82) | copy-start | bytes 36868
  92.5 8.9 %copy-start.34 = (f32[1,768]{1,0:T(1,128)S(1)}, f32[1,768]{1,0:T(1,128)}, u32[]{:S(2)}) copy-start(f32[1,768]{1,0:T(1,128)} %broadcast_in_dim.88) | copy-start | bytes 9220
  136.6 4.9 %copy-start.2 = (f32[768,384]{1,0:T(8,128)S(1)}, f32[768,384]{1,0:T(8,128)}, u32[]{:S(2)}) copy-start(f32[768,384]{1,0:T(8,128)} %copy-done.1) | copy-start | bytes 3538948
  (13 other events, 11.5 us)

commit v2 on v1

--- a/solution.py
+++ b/solution.py
@@ -320,131 +320,270 @@
     )(outbound, w_in, w_out)
 
 
-def final_kernel(n_ex, *refs):
-    (qkv, out, small, qkv_o, out_o, small_o, ql, ol, qs, os_, qx, ox,
-     qf, of_, sl, sx, sc, sa, sb,
-     rsend, rrecv, esend, erecv, asend, arecv, csend, crecv) = refs
+def bias_of(line, rows, cols):
+    return pltpu.roll(
+        jnp.broadcast_to(line, (rows, line.shape[1])), 0, 1, stride=1, stride_axis=0
+    )[:, :cols]
+
+
+def diagonals_of(matrix, span):
+    rows, cols = matrix.shape
+    wide = jnp.concatenate([matrix, jnp.zeros((rows, span - cols), matrix.dtype)], axis=1)
+    acc = wide[:8]
+    for tile in range(1, rows // 8):
+        acc = acc + pltpu.roll(wide[8 * tile : 8 * tile + 8], span - 8 * tile, 1)
+    line = acc[:1]
+    for row in range(1, 8):
+        line = line + pltpu.roll(acc[row : row + 1], span - row, 1)
+    return line
+
+
+def back_kernel(n_ex, n_col, heads, *refs):
+    (sg, sgf, attn, outw, q, k, v, level, lines, seg_q, seg_k, xn, unit, qkvw, small, rows_t,
+     unit_q, inv_q, gain, input_o, qkv_o, out_o, small_o,
+     ba, prob_s, kvb, kvl, st, tb, tl, qs, qx, qf, ob, ol, os_, ox, of_, xb, xl,
+     sa, sl, sx, sb, sc,
+     bs, br, ks, kr, ts, tr, qss, qsr, qas, qar, os1, or1, os2, or2, os3, or3,
+     xs, xr, ss1, sr1, ss2, sr2, ss3, sr3) = refs
     bf16, f32 = jnp.bfloat16, jnp.float32
     ex, row, col = lax.axis_index("ex"), lax.axis_index("row"), lax.axis_index("col")
     ex_peers, col_peers = others("ex"), others("col")
     mate = {"row": 1 - row}
-    greet([{"ex": p} for p in ex_peers] + [{"col": p} for p in col_peers] + [mate])
-    waits = []
-    one = [
-        remote(small, sl, rsend.at[2], rrecv.at[2], mate),
-        remote(qkv.at[1 - row], ql, rsend.at[0], rrecv.at[0], mate),
-        remote(out.at[1 - row], ol, rsend.at[1], rrecv.at[1], mate),
-    ]
-    for copy in one:
-        copy.start()
-    one[0].wait_recv()
-    sa[...] = small[...] + sl[...]
-    small_ex = [
-        remote(sa, sx.at[k], esend.at[2, k], erecv.at[2, k], {"ex": p})
-        for k, p in enumerate(ex_peers)
-    ]
-    for copy in small_ex:
-        copy.start()
-    one[1].wait_recv()
-    qs[...] = (qkv[row].astype(f32) + ql[...].astype(f32)).astype(bf16).reshape(qs.shape)
-    q_ex = [
-        remote(qs.at[p], qx.at[k], esend.at[0, k], erecv.at[0, k], {"ex": p})
-        for k, p in enumerate(ex_peers)
-    ]
-    for copy in q_ex:
-        copy.start()
-    one[2].wait_recv()
-    os_[...] = (out[row].astype(f32) + ol[...].astype(f32)).astype(bf16).reshape(os_.shape)
-    o_ex = [
-        remote(os_.at[p], ox.at[k], esend.at[1, k], erecv.at[1, k], {"ex": p})
-        for k, p in enumerate(ex_peers)
-    ]
-    for copy in o_ex:
-        copy.start()
-    total = sa[...]
-    for k, copy in enumerate(small_ex):
+    greet([{"col": p} for p in col_peers] + [{"ex": p} for p in ex_peers] + [mate])
+    everything = []
+
+    def go(copies):
+        for copy in copies:
+            copy.start()
+        everything.extend(copies)
+        return copies
+
+    first = go(
+        [remote(sg, ba.at[col], bs.at[i], br.at[i], {"col": p}) for i, p in enumerate(col_peers)]
+    )
+    ba[col] = sg[...]
+    count, width = xn.shape
+    group = k.shape[1]
+    span = lines.shape[2]
+    half = width // 2
+    scale = HDIM ** (-0.5)
+    same = seg_q[...] == seg_k[...]
+    for h in range(heads):
+        raw = lax.dot_general(q[h], k[h], INNER, preferred_element_type=f32)
+        raw = raw * scale + bias_of(lines[h], count, group)
+        prob_s[h] = jnp.exp(jnp.where(same, raw, NEG) - level[h])
+    for copy in first:
         copy.wait_recv()
-        total = total + sx[k]
-    sb[...] = total
-    small_col = [
-        remote(sb, sc.at[k], csend.at[k], crecv.at[k], {"col": p})
-        for k, p in enumerate(col_peers)
-    ]
-    for copy in small_col:
-        copy.start()
-    total = qs[ex].astype(f32)
-    for k, copy in enumerate(q_ex):
+    branch = ba[...].reshape(count, width)
+    d_attn = lax.dot_general(branch, outw[...], INNER, preferred_element_type=f32).astype(bf16)
+    out_full = lax.dot_general(attn[...], branch, OUTER, preferred_element_type=f32).astype(bf16)
+    ob[0] = out_full[:, :half]
+    ob[1] = out_full[:, half:]
+    out_one = go([remote(ob.at[1 - row], ol, os1.at[0], or1.at[0], mate)])
+
+    d_query, diags, kv_copies, t_copies, q_copies, a_copies = {}, [], {}, {}, {}, {}
+
+    def head(h):
+        prob = prob_s[h]
+        g = d_attn[:, h * HDIM : (h + 1) * HDIM]
+        d_prob = lax.dot_general(g, v[h], INNER, preferred_element_type=f32)
+        mean = jnp.sum(d_prob * prob, axis=1, keepdims=True)
+        ds = (prob * (d_prob - mean)).astype(bf16)
+        d_key = lax.dot_general(ds, q[h], OUTER, preferred_element_type=f32) * scale
+        d_val = lax.dot_general(prob.astype(bf16), g, OUTER, preferred_element_type=f32)
+        kvb[h] = (
+            jnp.concatenate([d_key, d_val], axis=1).astype(bf16).reshape(2, count, 2 * HDIM)
+        )
+        kv_copies[h] = go([remote(kvb.at[h, 1 - row], kvl.at[h], ks.at[h], kr.at[h], mate)])
+        d_query[h] = jnp.dot(ds, k[h], preferred_element_type=f32) * scale
+        diags.append(diagonals_of(ds.astype(f32), span))
+
+    def finish(h):
+        kv_copies[h][0].wait_recv()
+        pair = kvb[h, row].astype(f32) + kvl[h].astype(f32)
+        rows = jnp.concatenate([d_query[h], pair], axis=1).astype(bf16)
+        st[h] = rows
+        full = lax.dot_general(rows, xn[...], OUTER, preferred_element_type=f32).astype(bf16)
+        tb[h, 0] = full[:, :half]
+        tb[h, 1] = full[:, half:]
+        t_copies[h] = go([remote(tb.at[h, 1 - row], tl.at[h], ts.at[h], tr.at[h], mate)])
+
+    def second(h):
+        t_copies[h][0].wait_recv()
+        both = tb[h, row].astype(f32) + tl[h].astype(f32)
+        qs[h] = both.astype(bf16).reshape(qs.shape[1:])
+        q_copies[h] = go(
+            [
+                remote(qs.at[h, p], qx.at[h, i], qss.at[h, i], qsr.at[h, i], {"ex": p})
+                for i, p in enumerate(ex_peers)
+            ]
+        )
+
+    def third(h):
+        total = qs[h, ex].astype(f32)
+        for i, copy in enumerate(q_copies[h]):
+            copy.wait_recv()
+            total = total + qx[h, i].astype(f32)
+        qf[h, ex] = total.astype(bf16)
+        a_copies[h] = go(
+            [
+                remote(qf.at[h, ex], qf.at[h, ex], qas.at[h, i], qar.at[h, i], {"ex": p})
+                for i, p in enumerate(ex_peers)
+            ]
+        )
+
+    head(0)
+    for h in range(1, heads):
+        head(h)
+        if h >= 2:
+            second(h - 2)
+        finish(h - 1)
+        if h == 1:
+            out_one[0].wait_recv()
+            both = ob[row].astype(f32) + ol[...].astype(f32)
+            os_[...] = both.astype(bf16).reshape(os_.shape)
+            out_two = go(
+                [
+                    remote(os_.at[p], ox.at[i], os2.at[i], or2.at[i], {"ex": p})
+                    for i, p in enumerate(ex_peers)
+                ]
+            )
+    finish(heads - 1)
+    second(heads - 2)
+    rows = jnp.concatenate([st[h] for h in range(heads)], axis=1)
+    d_xn = lax.dot_general(rows, qkvw[...], INNER, preferred_element_type=f32)
+    xb[...] = d_xn.astype(bf16).reshape(xb.shape)
+    x_copies = go(
+        [remote(xb.at[p], xl.at[i], xs.at[i], xr.at[i], {"col": p}) for i, p in enumerate(col_peers)]
+    )
+    second(heads - 1)
+    norm = jnp.sum(d_xn * unit[...], axis=0, keepdims=True)
+    diag = jnp.concatenate(diags + [jnp.zeros((8 - heads, span), f32)], axis=0)
+    table = jnp.dot(diag, rows_t[...], precision=HIGH, preferred_element_type=f32)
+    spot = lax.broadcasted_iota(jnp.int32, small.shape, 0)
+    sa[:, :width] = jnp.where(spot == 0, norm, small[...])
+    sa[:, width:] = table
+    small_one = go([remote(sa, sl, ss1.at[0], sr1.at[0], mate)])
+    third(0)
+    small_one[0].wait_recv()
+    sb[0] = sa[...] + sl[...]
+    small_two = go(
+        [
+            remote(sb.at[0], sx.at[i], ss2.at[i], sr2.at[i], {"ex": p})
+            for i, p in enumerate(ex_peers)
+        ]
+    )
+    total = os_[ex].astype(f32)
+    for i, copy in enumerate(out_two):
         copy.wait_recv()
-        total = total + qx[k].astype(f32)
-    qf[ex] = total.astype(bf16)
-    gathers = [
-        remote(qf.at[ex], qf.at[ex], asend.at[0, k], arecv.at[0, k], {"ex": p})
-        for k, p in enumerate(ex_peers)
-    ]
-    for copy in gathers:
-        copy.start()
-    total = os_[ex].astype(f32)
-    for k, copy in enumerate(o_ex):
+        total = total + ox[i].astype(f32)
+    of_[ex] = total.astype(bf16)
+    out_three = go(
+        [
+            remote(of_.at[ex], of_.at[ex], os3.at[i], or3.at[i], {"ex": p})
+            for i, p in enumerate(ex_peers)
+        ]
+    )
+    third(1)
+    d_own = xb[col].astype(f32)
+    for i, copy in enumerate(x_copies):
         copy.wait_recv()
-        total = total + ox[k].astype(f32)
-    of_[ex] = total.astype(bf16)
-    more = [
-        remote(of_.at[ex], of_.at[ex], asend.at[1, k], arecv.at[1, k], {"ex": p})
-        for k, p in enumerate(ex_peers)
-    ]
-    for copy in more:
-        copy.start()
-    whole = sb[...]
-    for k, copy in enumerate(small_col):
+        d_own = d_own + xl[i].astype(f32)
+    scaled = gain[...] * d_own
+    inner = jnp.sum(scaled * unit_q[...], axis=1, keepdims=True) * (1.0 / width)
+    input_o[...] = sgf[...] + inv_q[...] * (scaled - unit_q[...] * inner)
+    for h in range(2, heads):
+        third(h)
+    total = sb[0]
+    for i, copy in enumerate(small_two):
         copy.wait_recv()
-        whole = whole + sc[k]
-    spot = lax.broadcasted_iota(jnp.int32, whole.shape, 0)
-    small_o[...] = jnp.where(spot == 0, sb[...], whole)
-    for copy in gathers:
-        copy.wait_recv()
-    qkv_o[...] = qf[...].astype(f32).reshape(qkv_o.shape)
-    for copy in more:
+        total = total + sx[i]
+    sb[1] = total
+    small_three = go(
+        [
+            remote(sb.at[1], sc.at[i], ss3.at[i], sr3.at[i], {"col": p})
+            for i, p in enumerate(col_peers)
+        ]
+    )
+    for copy in out_three:
         copy.wait_recv()
     out_o[...] = of_[...].astype(f32).reshape(out_o.shape)
-    for copy in one + small_ex + q_ex + o_ex + small_col + gathers + more:
+    for i, copy in enumerate(small_three):
+        copy.wait_recv()
+        total = total + sc[i]
+    small_o[:, :width] = total[:, :width]
+    small_o[:, width:] = sb[1, :, width:]
+    for h in range(heads):
+        for copy in a_copies[h]:
+            copy.wait_recv()
+        piece = qf[h].astype(f32).reshape(3 * HDIM, half)
+        qkv_o[:, h * 3 * HDIM : (h + 1) * 3 * HDIM] = piece.T
+    for copy in everything:
         copy.wait_send()
 
 
-def final_sums(qkv, out, small):
+def back_block(sg, sgf, attn, outw, q, k, v, level, lines, seg_q, seg_k, xn, unit, qkvw, small,
+               rows_t, unit_q, inv_q, gain):
     n_ex, n_col = lax.axis_size("ex"), lax.axis_size("col")
     bf16, f32 = jnp.bfloat16, jnp.float32
-    _, qr, qc = qkv.shape
-    _, orr, oc = out.shape
+    heads, group, _ = k.shape
+    count, width = xn.shape
+    quarter = sg.shape[0]
+    half = width // 2
+    tri = 3 * HDIM
+    wide = width + rows_t.shape[1]
+    head_rows = outw.shape[0]
+    args = (sg, sgf, attn, outw, q, k, v, level, lines, seg_q, seg_k, xn, unit, qkvw, small,
+            rows_t, unit_q, inv_q, gain)
+    V = pltpu.VMEM
     return pl.pallas_call(
-        lambda *refs: final_kernel(n_ex, *refs),
+        lambda *refs: back_kernel(n_ex, n_col, heads, *refs),
         out_shape=(
-            jax.ShapeDtypeStruct((qr, qc), f32),
-            jax.ShapeDtypeStruct((orr, oc), f32),
-            jax.ShapeDtypeStruct(small.shape, f32),
+            jax.ShapeDtypeStruct((quarter, width), f32),
+            jax.ShapeDtypeStruct((half, heads * tri), f32),
+            jax.ShapeDtypeStruct((head_rows, half), f32),
+            jax.ShapeDtypeStruct((8, wide), f32),
         ),
-        in_specs=[VMEM] * 3,
-        out_specs=(VMEM,) * 3,
+        in_specs=[VMEM] * len(args),
+        out_specs=(VMEM,) * 4,
         scratch_shapes=[
-            pltpu.VMEM((qr, qc), bf16),
-            pltpu.VMEM((orr, oc), bf16),
-            pltpu.VMEM((n_ex, qr // n_ex, qc), bf16),
-            pltpu.VMEM((n_ex, orr // n_ex, oc), bf16),
-            pltpu.VMEM((n_ex - 1, qr // n_ex, qc), bf16),
-            pltpu.VMEM((n_ex - 1, orr // n_ex, oc), bf16),
-            pltpu.VMEM((n_ex, qr // n_ex, qc), bf16),
-            pltpu.VMEM((n_ex, orr // n_ex, oc), bf16),
-            pltpu.VMEM(small.shape, f32),
-            pltpu.VMEM((n_ex - 1, *small.shape), f32),
-            pltpu.VMEM((n_col - 1, *small.shape), f32),
-            pltpu.VMEM(small.shape, f32),
-            pltpu.VMEM(small.shape, f32),
-            DMA((3,)), DMA((3,)),
-            DMA((3, n_ex - 1)), DMA((3, n_ex - 1)),
-            DMA((2, n_ex - 1)), DMA((2, n_ex - 1)),
+            V((n_col, quarter, width), bf16),
+            V((heads, count, group), f32),
+            V((heads, 2, count, 2 * HDIM), bf16),
+            V((heads, count, 2 * HDIM), bf16),
+            V((heads, count, tri), bf16),
+            V((heads, 2, tri, half), bf16),
+            V((heads, tri, half), bf16),
+            V((heads, n_ex, tri // n_ex, half), bf16),
+            V((heads, n_ex - 1, tri // n_ex, half), bf16),
+            V((heads, n_ex, tri // n_ex, half), bf16),
+            V((2, head_rows, half), bf16),
+            V((head_rows, half), bf16),
+            V((n_ex, head_rows // n_ex, half), bf16),
+            V((n_ex - 1, head_rows // n_ex, half), bf16),
+            V((n_ex, head_rows // n_ex, half), bf16),
+            V((n_col, quarter, width), bf16),
+            V((n_col - 1, quarter, width), bf16),
+            V((8, wide), f32),
+            V((8, wide), f32),
+            V((n_ex - 1, 8, wide), f32),
+            V((2, 8, wide), f32),
+            V((n_col - 1, 8, wide), f32),
+            DMA((n_col - 1,)), DMA((n_col - 1,)),
+            DMA((heads,)), DMA((heads,)),
+            DMA((heads,)), DMA((heads,)),
+            DMA((heads, n_ex - 1)), DMA((heads, n_ex - 1)),
+            DMA((heads, n_ex - 1)), DMA((heads, n_ex - 1)),
+            DMA((1,)), DMA((1,)),
+            DMA((n_ex - 1,)), DMA((n_ex - 1,)),
+            DMA((n_ex - 1,)), DMA((n_ex - 1,)),
+            DMA((n_col - 1,)), DMA((n_col - 1,)),
+            DMA((1,)), DMA((1,)),
+            DMA((n_ex - 1,)), DMA((n_ex - 1,)),
             DMA((n_col - 1,)), DMA((n_col - 1,)),
         ],
         compiler_params=params(8),
-    )(qkv, out, small)
+    )(*args)
 
 
 def expert_exchange(outbound, w_in, w_out):
@@ -521,7 +660,7 @@
     segment = jnp.sum((places[:, None] >= ends[None, :]).astype(jnp.int32), axis=1)
     own_segment = lax.dynamic_slice_in_dim(segment, local_offset, tokens_per_device, 0)
     same = own_segment[:, None] == segment[None, :]
-    span = tokens_per_device + group - 1
+    span = -(-(tokens_per_device + group - 1) // 128) * 128
     offsets = jnp.arange(span, dtype=jnp.int32)
     shifts = jnp.where(offsets < group, offsets, offsets - span) - local_offset
     table_rows = (
@@ -614,6 +753,57 @@
         - second_unit_input
         * jnp.mean(second_scaled_input * second_unit_input, axis=1, keepdims=True)
     )
+    xn_own = lax.dynamic_slice_in_dim(first_normed_input, local_offset, tokens_per_device, 0)
+    local_unit_input = lax.dynamic_slice_in_dim(
+        first_unit_input, local_offset, tokens_per_device, 0
+    )
+    quarter_unit_input = lax.dynamic_slice_in_dim(
+        local_unit_input, quarter_offset, dispatch_mask, 0
+    )
+    inv_quarter = lax.dynamic_slice_in_dim(
+        first_inverse_norm, local_offset + quarter_offset, dispatch_mask, 0
+    )
+    if direct:
+        small = jnp.concatenate(
+            [jnp.zeros((1, width), jnp.float32), second_norm_slice[None], router_part.T], axis=0
+        )
+        small = jnp.pad(small, ((0, 8 - small.shape[0]), (0, 0)))
+        input_grad, qkv_grad, out_grad, small = back_block(
+            state_grad.astype(jnp.bfloat16),
+            state_grad,
+            attn,
+            out_rows,
+            queries,
+            keys,
+            values,
+            log_total,
+            bias_lines[:, None, :],
+            own_segment[:, None],
+            segment[None, :],
+            xn_own,
+            local_unit_input,
+            qkv_rows,
+            small,
+            jnp.pad(table_rows, ((0, 0), (0, 128 - buckets))),
+            quarter_unit_input,
+            inv_quarter,
+            first_norm_scale[None, :],
+        )
+        norm1_grad, norm2_grad = small[0, :width], small[1, :width]
+        router_grad = small[2 : 2 + experts, :width].T
+        table_grad = small[:heads, width : width + buckets].T
+        return (
+            output,
+            input_grad,
+            qkv_grad,
+            out_grad,
+            table_grad,
+            norm1_grad,
+            norm2_grad,
+            router_grad,
+            inner_grad[None],
+            outer_grad[None],
+        )
     branch_all = gather_blocks(state_grad.astype(jnp.bfloat16), "col", 5).reshape(
         tokens_per_device, width
     )
@@ -660,10 +850,6 @@
         axis=2,
     )
     stacked = stacked.reshape(tokens_per_device, 3 * heads * HDIM).astype(jnp.bfloat16)
-    xn_own = lax.dynamic_slice_in_dim(first_normed_input, local_offset, tokens_per_device, 0)
-    local_unit_input = lax.dynamic_slice_in_dim(
-        first_unit_input, local_offset, tokens_per_device, 0
-    )
     qkv_full = lax.dot_general(xn_own, stacked, OUTER, preferred_element_type=jnp.float32)
     first_normed_slice = lax.dot_general(
         stacked, qkv_rows, INNER, preferred_element_type=jnp.float32
@@ -672,12 +858,6 @@
     table_part = jnp.dot(table_rows.T, diagonals.T, precision=HIGH)
     xn_one_grad = scatter_sum(
         first_normed_slice.astype(jnp.bfloat16).reshape(n_col, dispatch_mask, width), "col", 7
-    )
-    quarter_unit_input = lax.dynamic_slice_in_dim(
-        local_unit_input, quarter_offset, dispatch_mask, 0
-    )
-    inv_quarter = lax.dynamic_slice_in_dim(
-        first_inverse_norm, local_offset + quarter_offset, dispatch_mask, 0
     )
     first_scaled_input = first_norm_scale * xn_one_grad
     input_grad = state_grad + inv_quarter * (
@@ -686,26 +866,12 @@
         * jnp.mean(first_scaled_input * quarter_unit_input, axis=1, keepdims=True)
     )
     half = width // lax.axis_size("row")
-    if direct:
-        flat = jnp.pad(table_part.reshape(1, -1), ((0, 0), (0, width - buckets * heads)))
-        small = jnp.concatenate(
-            [flat, first_norm_slice[None], second_norm_slice[None], router_part.T], axis=0
-        )
-        small = jnp.pad(small, ((0, -small.shape[0] % 8), (0, 0)))
-        qkv_grad, out_grad, small = final_sums(
-            qkv_full.astype(jnp.bfloat16).reshape(2, half, -1),
-            out_full.astype(jnp.bfloat16).reshape(-1, 2, half).transpose(1, 0, 2),
-            small,
-        )
-        table_grad = small[0, : buckets * heads].reshape(buckets, heads)
-        norm1_grad, norm2_grad, router_grad = small[1], small[2], small[3 : 3 + experts].T
-    else:
-        qkv_sum, out_sum, table_grad = lax.psum((qkv_full, out_full, table_part), ("ex", "row"))
-        norm1_grad, norm2_grad, router_grad = lax.psum(
-            (first_norm_slice, second_norm_slice, router_part), ("ex", "row", "col")
-        )
-        qkv_grad = lax.dynamic_slice_in_dim(qkv_sum, my_row * half, half, 0)
-        out_grad = lax.dynamic_slice_in_dim(out_sum, my_row * half, half, 1)
+    qkv_sum, out_sum, table_grad = lax.psum((qkv_full, out_full, table_part), ("ex", "row"))
+    norm1_grad, norm2_grad, router_grad = lax.psum(
+        (first_norm_slice, second_norm_slice, router_part), ("ex", "row", "col")
+    )
+    qkv_grad = lax.dynamic_slice_in_dim(qkv_sum, my_row * half, half, 0)
+    out_grad = lax.dynamic_slice_in_dim(out_sum, my_row * half, half, 1)
     return (
         output,
         input_grad,

time: 144 us -> 131 us (0.910)
  Pallas kernels: 89.3 us -> 82 us
  matrix products: 15 us -> 9.59 us
  local copies, waits for them, and re-layouts: 29.4 us -> 31.5 us
  other arithmetic: 7.78 us -> 5.7 us
    unnamed x80 -> x68, local copies, waits for them, and re-layouts: 9.17 us -> 18.1 us
    pallas_call x3 -> x1, Pallas kernels: 16.7 us -> 8.36 us  [scatter_sum(): pl.pallas_call(kernel, out_shape=jax.ShapeDtypeStruct(blocks.shape[1:], j...]
    dot_general x17 -> x0, matrix products: 7.5 us -> none  [the longest x3 3.77 us: attend_back(): jnp.einsum('qd,kd->qk', grad, value, preferred_element_type=jnp.float32)]
    reshape x11 -> x0, local copies, waits for them, and re-layouts: 4.28 us -> none  [the longest x3 1.55 us: diagonal_sums(): padded = jnp.pad(matrix, ((0, 0), (0, span - 1 - cols))).reshape(-1)]
    dynamic_slice x3 -> x4, local copies, waits for them, and re-layouts: 2.06 us -> 4.7 us  [the longest x2 2.61 us: on_device(): lax.dynamic_slice_in_dim(first_inverse_norm, local_offset + quarter_offse...]
    another operation x12 -> x6, local copies, waits for them, and re-layouts: 2.56 us -> 0.2 us  [toeplitz(): tiled = jnp.tile(vector, rows)[:rows * (span - 1)]]
    broadcast_in_dim x4, local copies, waits for them, and re-layouts: 0.02 us -> 1.98 us  [the longest x1 0.69 us: on_device(): first_unit_input * first_norm_scale]
    add x1 -> x0, other arithmetic: 1.74 us -> none  [on_device(): state_grad + inv_quarter * (first_scaled_input - quarter_unit_input * jnp...]
where the time goes in v2:
time: 131 us; the launch traced here: 130 us
  Pallas kernels  82 us (63%)
  local copies, waits for them, and re-layouts  31.5 us (24%)
  matrix products  9.59 us (7%)
  other arithmetic  5.7 us (4%)
    pallas_call x1, Pallas kernels, back_block(): pl.pallas_call(lambda *refs: back_kernel(n_ex, n_col, heads, *refs), out_...  40.6 us
    pallas_call x1, Pallas kernels, expert_block(): pl.pallas_call(lambda *refs: expert_kernel(n_ex, n_col, cap, *refs), out_...  30.4 us
    unnamed x68, local copies, waits for them, and re-layouts  18.1 us
    pallas_call x1, Pallas kernels, scatter_sum(): pl.pallas_call(kernel, out_shape=jax.ShapeDtypeStruct(blocks.shape[1:], j...  8.36 us
    dot_general x3, matrix products, scores_of(): jnp.einsum('qd,kd->qk', query, key, preferred_element_type=jnp.float32)  3.34 us
    pallas_call x1, Pallas kernels, gather_row(): pl.pallas_call(kernel, out_shape=(jax.ShapeDtypeStruct((2 * rows, qkv_col...  2.63 us

profile of v2, /device:TPU:0, one launch (start us, length us, event | category | flops | bytes accessed | tf_op | source)
XLA Modules:
  0.0 130.1 jit_solution(1484814844304908222)
XLA Ops:
  0.7 1.3 copy.35.w
  2.0 1.0 copy-done.8
  2.9 0.9 copy-done.11
  3.8 2.6 %shard_map.204 = (bf16[768,576]{1,0:T(8,128)(2,1)S(1)}, bf16[192,768]{1,0:T(8,128)(2,1)S(1)}, bf16[384,768]{1,0:T(8,128)(2,1)S(1)}) custom-call(bf16[384,576]{1,0:T(8,128)(2,1)S(1)} %copy.35.w, bf16[192,384]{1,0:T(8,128)(2,1)S(1)} %copy-done.11, bf16[192,768]{1,0:T(8,128)(2,1)S(1)} %copy-done.8), custom_call_target="tpu_custom_call" | custom-call | tf_op jit(solution)/shard_map/pallas_call | solution.py:166
  6.7 1.2 convert_multiply_fusion
  7.9 0.7 convolution_convert_fusion
  9.2 0.7 dynamic-slice_bitcast_fusion.refs_4_
  10.7 6.9 %while.13 = (s32[]{:T(128)}, bf16[3,192,64]{1,2,0:T(8,128)(2,1)S(1)}, f32[3,192,1]{1,2,0:T(1,128)S(1)}, bf16[3,192,64]{2,1,0:T(8,128)(2,1)}, bf16[3,384,64]{2,1,...) while((s32[]{:T(128)}, ...), condition=%wide.region_6.7_spmd.clone, body=%wide.region_3.6_spmd.clone.sunk | while | flops 19611456 | bytes 3968629 | solution.py:687
  11.3 1.1 fusion.75
  13.1 0.5 reshape.190
  13.6 1.1 fusion.75
  15.9 1.1 fusion.75
  17.7 0.6 copy-done.20
  18.7 8.4 %shard_map.205 = f32[48,768]{1,0:T(8,128)S(1)} custom-call(bf16[4,48,768]{2,1,0:T(8,128)(2,1)S(1)} %bitcast.77), custom_call_target="tpu_custom_call" | custom-call | tf_op jit(solution)/shard_map/pallas_call | solution.py:127
  27.0 1.0 multiply_reduce_fusion.2
  28.5 1.1 convolution_convert_fusion.2
  29.8 1.1 copy-done.7
  30.9 30.4 %shard_map.206 = (bf16[4,32,768]{2,1,0:T(8,128)(2,1)S(1)}, f32[768,384]{1,0:T(8,128)S(1)}, f32[384,768]{1,0:T(8,128)S(1)}) custom-call(bf16[4,32,768]{2,1,0:T(8,128)(2,1)S(1)} %pad_maximum_fusion.refs_0_, bf16[768,384]{1,0:T(8,128)(2,1)S(1)} %bitcast.78, bf16[384,768]{1,0:T(8,128)(2,1)S(1)} %bitcast.79), custom_call_target="tpu_custom_call" | custom-call | tf_op jit(solution)/shard_map/pallas_call | solution.py:292
  61.3 1.3 fusion.18
  62.9 1.0 multiply_reduce_fusion
  63.9 1.8 %fusion.53 = (bf16[48,768]{1,0:T(8,128)(2,1)S(1)}, f32[48,768]{1,0:T(8,128)S(1)}, f32[48,768]{1,0:T(8,128)}, f32[48,768]{1,0:T(8,128)S(1)}) fusion(f32[48]{0:T(128)S(1)} %broadcast_multiply_fusion, f32[48,768]{1,0:T(8,128)S(1)} %get-tuple-element.154, f32[48,768]{1,0:T(8,128)} %get-tuple-element.171, f32[768]{0:T(1024)S(1)} %copy-done.24, ...), kind=kLoop, calls=%fused_computation.104 | loop fusion | flops 368640 | bytes 1183304 | tf_op jit(solution)/shard_map/convert_element_type | solution.py:772
  65.7 1.0 copy.37.refs_2_
  66.9 0.6 broadcast_in_dim.34.refs_8_
  67.6 0.6 broadcast_in_dim.36.refs_10_
  68.2 1.0 constant_dynamic-slice_fusion.2.refs_11_
  69.2 1.1 constant_dynamic-slice_fusion.1.refs_12_
  70.6 0.6 pad.10.refs_14_
  71.4 1.3 dynamic-slice_bitcast_fusion.1
  72.6 1.3 %copy.40.refs_17_ = f32[48,1]{1,0:T(8,128)} copy(f32[48,1]{0,1:T(1,128)} %dynamic-slice_bitcast_fusion.1) | data formatting | bytes 384 | tf_op jit(solution)/shard_map/dynamic_slice | solution.py:763
  74.0 0.7 broadcast_in_dim.39.refs_18_
  74.7 1.2 copy-done.5
  75.9 0.7 copy-done.14
  76.6 0.7 copy-done.15
  77.4 0.7 copy-done.16
  78.1 0.7 copy-done.19
  78.7 40.6 %shard_map.207 = (f32[48,768]{1,0:T(8,128)S(1)}, f32[384,576]{1,0:T(8,128)S(1)}, f32[192,384]{1,0:T(8,128)S(1)}, f32[8,896]{1,0:T(8,128)S(1)}) custom-call(bf16[48,768]{1,0:T(8,128)(2,1)S(1)} %get-tuple-element.149.refs_0_, f32[48,768]{1,0:T(8,128)S(1)} %get-tuple-element.150.refs_1_, bf16[192,192]{1,0:T(8,128)(2,1)S(1)} %copy.37.refs_2_, ...), custom_call_target="tpu_custom_call" | custom-call | tf_op jit(solution)/shard_map/pallas_call | solution.py:539
  119.4 0.9 copy-done.3
  120.3 0.7 copy-done.9
  121.0 0.7 copy-done.12
  121.7 0.6 copy-done.17
  122.3 2.6 %copy.41 = f32[384,576]{0,1:T(8,128)} copy(f32[384,576]{1,0:T(8,128)} %copy-done.3) | data formatting | bytes 1769472
  124.9 0.6 slice_bitcast_fusion.3
  125.4 0.6 slice_reduce_fusion
  126.1 0.6 slice_bitcast_fusion.2
  126.7 0.7 copy.57
  127.3 0.7 copy.58
  128.0 1.0 copy.59
  129.1 1.0 copy.60
  (104 shorter events, 6.5 us)
Async XLA Ops:
  0.6 27.6 %copy-start = (bf16[768,4]{0,1:T(4,128)(2,1)S(1)}, bf16[768,4]{0,1:T(4,128)(2,1)}, u32[]{:S(2)}) copy-start(bf16[768,4]{0,1:T(4,128)(2,1)} %param.21) | copy-start | bytes 18436
  0.7 6.0 %copy-start.25 = (f32[768]{0:T(1024)S(1)}, f32[768]{0:T(1024)}, u32[]{:S(2)}) copy-start(f32[768]{0:T(1024)} %param.19) | copy-start | bytes 9220
  2.0 1.0 copy-start.8
  2.9 0.9 copy-start.11
  6.5 1.5 %copy-start.4 = (bf16[768,576]{1,0:T(8,128)(2,1)}, bf16[768,576]{1,0:T(8,128)(2,1)S(1)}, u32[]{:S(2)}) copy-start(bf16[768,576]{1,0:T(8,128)(2,1)S(1)} %get-tuple-element.64.refs_13_) | copy-start | bytes 2654212
  6.7 1.2 copy-start.26
  7.9 0.8 copy-start.21
  9.2 0.8 copy-start.29
  9.2 1.1 copy-start.30
  17.6 0.7 copy-start.20
  17.6 0.8 copy-start.22
  17.6 12.0 %copy-start.23 = (bf16[3,192,64]{1,2,0:T(8,128)(2,1)}, bf16[3,192,64]{1,2,0:T(8,128)(2,1)S(1)}, u32[]{:S(2)}) copy-start(bf16[3,192,64]{1,2,0:T(8,128)(2,1)S(1)} %get-tuple-element.65) | copy-start | bytes 221188
  17.6 10.5 %copy-start.27 = (s32[192]{0:T(256)S(1)}, s32[192]{0:T(256)}, u32[]{:S(2)}) copy-start(s32[192]{0:T(256)} %param.26) | copy-start | bytes 2308
  17.6 10.5 %copy-start.28 = (s32[192]{0:T(256)S(1)}, s32[192]{0:T(256)}, u32[]{:S(2)}) copy-start(s32[192]{0:T(256)} %param.25) | copy-start | bytes 2308
  17.6 10.5 %copy-start.24 = (f32[768]{0:T(1024)S(1)}, f32[768]{0:T(1024)}, u32[]{:S(2)}) copy-start(f32[768]{0:T(1024)} %param.20) | copy-start | bytes 9220
  18.4 11.4 %copy-start.6 = (bf16[1,768,384]{2,1,0:T(8,128)(2,1)S(1)}, bf16[1,768,384]{2,1,0:T(8,128)(2,1)}, u32[]{:S(2)}) copy-start(bf16[1,768,384]{2,1,0:T(8,128)(2,1)} %param.22) | copy-start | bytes 1769476
  29.8 1.1 copy-start.7
  61.3 4.5 %copy-start.1 = (f32[768,384]{1,0:T(8,128)}, f32[768,384]{1,0:T(8,128)S(1)}, u32[]{:S(2)}) copy-start(f32[768,384]{1,0:T(8,128)S(1)} %get-tuple-element.73) | copy-start | bytes 3538948
  74.7 1.2 copy-start.5
  75.9 0.7 copy-start.14
  76.6 0.7 copy-start.15
  77.4 0.7 copy-start.16
  78.1 0.7 copy-start.19
  119.4 0.9 copy-start.3
  120.3 0.7 copy-start.9
  121.0 0.7 copy-start.12
  121.7 0.6 copy-start.17
  122.3 2.6 %copy-start.18 = (f32[8,896]{1,0:T(8,128)S(1)}, f32[8,896]{1,0:T(8,128)}, u32[]{:S(2)}) copy-start(f32[8,896]{1,0:T(8,128)} %copy-done.17) | copy-start | bytes 86020
  122.3 4.4 %copy-start.13 = (f32[48,768]{1,0:T(8,128)S(1)}, f32[48,768]{1,0:T(8,128)}, u32[]{:S(2)}) copy-start(f32[48,768]{1,0:T(8,128)} %copy-done.12) | copy-start | bytes 442372
  122.3 5.0 %copy-start.10 = (f32[192,384]{1,0:T(8,128)S(1)}, f32[192,384]{1,0:T(8,128)}, u32[]{:S(2)}) copy-start(f32[192,384]{1,0:T(8,128)} %copy-done.9) | copy-start | bytes 884740
  122.3 5.7 %copy-start.2 = (f32[768,384]{1,0:T(8,128)S(1)}, f32[768,384]{1,0:T(8,128)}, u32[]{:S(2)}) copy-start(f32[768,384]{1,0:T(8,128)} %copy-done.1) | copy-start | bytes 3538948

commit v3 on v2

--- a/solution.py
+++ b/solution.py
@@ -185,141 +185,6 @@
     return value, slope
 
 
-def expert_kernel(n_ex, n_col, cap, *refs):
-    (out_b, w_in, w_out, back, g_in, g_out, p_in, p_out, land, part, got, summed,
-     s_in, s_out, r_in, r_out, wsend, wrecv, xsend, xrecv, csend, crecv,
-     psend, precv, bsend, brecv, gsend, grecv) = refs
-    bf16, f32 = jnp.bfloat16, jnp.float32
-    ex, row, col = lax.axis_index("ex"), lax.axis_index("row"), lax.axis_index("col")
-    width = w_in.shape[0]
-    tokens = n_ex * n_col * cap
-    ex_peers, col_peers = others("ex"), others("col")
-    mate = {"row": 1 - row}
-    greet([{"ex": p} for p in ex_peers] + [{"col": p} for p in col_peers] + [mate])
-    first = [
-        remote(out_b.at[p], land.at[col, ex], xsend.at[k], xrecv.at[k], {"ex": p})
-        for k, p in enumerate(ex_peers)
-    ]
-    for copy in first:
-        copy.start()
-    weights = [
-        remote(w_in, p_in, wsend.at[0], wrecv.at[0], mate),
-        remote(w_out, p_out, wsend.at[1], wrecv.at[1], mate),
-    ]
-    land[col, ex] = out_b[ex]
-    spread = []
-
-    def forward(slot, index):
-        for k, p in enumerate(col_peers):
-            copy = remote(
-                land.at[col, slot], land.at[col, slot],
-                csend.at[index, k], crecv.at[index, k], {"col": p},
-            )
-            copy.start()
-            spread.append(copy)
-
-    forward(ex, 0)
-    for copy in weights:
-        copy.start()
-    for k, copy in enumerate(first):
-        copy.wait_recv()
-        forward(lax.rem(ex + n_ex - 1 - k, n_ex), 1 + k)
-    for copy in spread:
-        copy.wait_recv()
-    for copy in weights:
-        copy.wait()
-    x = land[:, :, :cap, :].reshape(tokens, width)
-    g = land[:, :, cap:, :].reshape(tokens, width)
-    y = jnp.zeros((tokens, width), f32)
-    d = jnp.zeros((tokens, width), f32)
-    kept = []
-    for wi, wo in ((w_in, w_out), (p_in, p_out)):
-        pre = jnp.dot(x, wi[...], preferred_element_type=f32)
-        value, slope = gelu_parts(pre)
-        hid = value.astype(bf16)
-        y = y + jnp.dot(hid, wo[...], preferred_element_type=f32)
-        d_hid = lax.dot_general(g, wo[...], INNER, preferred_element_type=f32)
-        d_pre = (d_hid * slope).astype(bf16)
-        d = d + lax.dot_general(d_pre, wi[...], INNER, preferred_element_type=f32)
-        kept.append((hid, d_pre))
-    part[:, :, :cap, :] = y.astype(bf16).reshape(n_col, n_ex, cap, width)
-    part[:, :, cap:, :] = d.astype(bf16).reshape(n_col, n_ex, cap, width)
-    sums = [
-        remote(part.at[p], got.at[k], psend.at[k], precv.at[k], {"col": p})
-        for k, p in enumerate(col_peers)
-    ]
-    for copy in sums:
-        copy.start()
-    s_in[...] = lax.dot_general(x, kept[1][1], OUTER, preferred_element_type=f32).astype(bf16)
-    s_out[...] = lax.dot_general(kept[1][0], g, OUTER, preferred_element_type=f32).astype(bf16)
-    grads = [
-        remote(s_in, r_in, gsend.at[0], grecv.at[0], mate),
-        remote(s_out, r_out, gsend.at[1], grecv.at[1], mate),
-    ]
-    for copy in grads:
-        copy.start()
-    for copy in sums:
-        copy.wait_recv()
-    total = part[col].astype(f32)
-    for k in range(n_col - 1):
-        total = total + got[k].astype(f32)
-    summed[...] = total.astype(bf16)
-    home = [
-        remote(summed.at[p], back.at[ex], bsend.at[k], brecv.at[k], {"ex": p})
-        for k, p in enumerate(ex_peers)
-    ]
-    for copy in home:
-        copy.start()
-    back[ex] = summed[ex]
-    g_in[...] = lax.dot_general(x, kept[0][1], OUTER, preferred_element_type=f32)
-    g_out[...] = lax.dot_general(kept[0][0], g, OUTER, preferred_element_type=f32)
-    for copy in grads:
-        copy.wait_recv()
-    g_in[...] += r_in[...].astype(f32)
-    g_out[...] += r_out[...].astype(f32)
-    for copy in home:
-        copy.wait()
-    for copy in first + spread + sums + grads:
-        copy.wait_send()
-
-
-def expert_block(outbound, w_in, w_out):
-    n_ex, twice, width = outbound.shape
-    n_col = lax.axis_size("col")
-    cap = twice // 2
-    bf16 = jnp.bfloat16
-    cols = w_in.shape[1]
-    return pl.pallas_call(
-        lambda *refs: expert_kernel(n_ex, n_col, cap, *refs),
-        out_shape=(
-            jax.ShapeDtypeStruct((n_ex, twice, width), bf16),
-            jax.ShapeDtypeStruct((width, cols), jnp.float32),
-            jax.ShapeDtypeStruct((cols, width), jnp.float32),
-        ),
-        in_specs=[VMEM] * 3,
-        out_specs=(VMEM,) * 3,
-        scratch_shapes=[
-            pltpu.VMEM((width, cols), bf16),
-            pltpu.VMEM((cols, width), bf16),
-            pltpu.VMEM((n_col, n_ex, twice, width), bf16),
-            pltpu.VMEM((n_col, n_ex, twice, width), bf16),
-            pltpu.VMEM((n_col - 1, n_ex, twice, width), bf16),
-            pltpu.VMEM((n_ex, twice, width), bf16),
-            pltpu.VMEM((width, cols), bf16),
-            pltpu.VMEM((cols, width), bf16),
-            pltpu.VMEM((width, cols), bf16),
-            pltpu.VMEM((cols, width), bf16),
-            DMA((2,)), DMA((2,)),
-            DMA((n_ex - 1,)), DMA((n_ex - 1,)),
-            DMA((n_ex, n_col - 1)), DMA((n_ex, n_col - 1)),
-            DMA((n_col - 1,)), DMA((n_col - 1,)),
-            DMA((n_ex - 1,)), DMA((n_ex - 1,)),
-            DMA((2,)), DMA((2,)),
-        ],
-        compiler_params=params(4),
-    )(outbound, w_in, w_out)
-
-
 def bias_of(line, rows, cols):
     return pltpu.roll(
         jnp.broadcast_to(line, (rows, line.shape[1])), 0, 1, stride=1, stride_axis=0
@@ -338,85 +203,225 @@
     return line
 
 
-def back_kernel(n_ex, n_col, heads, *refs):
-    (sg, sgf, attn, outw, q, k, v, level, lines, seg_q, seg_k, xn, unit, qkvw, small, rows_t,
-     unit_q, inv_q, gain, input_o, qkv_o, out_o, small_o,
-     ba, prob_s, kvb, kvl, st, tb, tl, qs, qx, qf, ob, ol, os_, ox, of_, xb, xl,
-     sa, sl, sx, sb, sc,
-     bs, br, ks, kr, ts, tr, qss, qsr, qas, qar, os1, or1, os2, or2, os3, or3,
-     xs, xr, ss1, sr1, ss2, sr2, ss3, sr3) = refs
+def whole_kernel(dims, names, *refs):
+    n_ex, n_col, heads, cap, buckets, count, width, quarter = dims
+    r = dict(zip(names, refs))
     bf16, f32 = jnp.bfloat16, jnp.float32
     ex, row, col = lax.axis_index("ex"), lax.axis_index("row"), lax.axis_index("col")
     ex_peers, col_peers = others("ex"), others("col")
     mate = {"row": 1 - row}
-    greet([{"col": p} for p in col_peers] + [{"ex": p} for p in ex_peers] + [mate])
+    group = 2 * count
+    half = width // 2
+    tri = 3 * HDIM
+    span = -(-(count + group - 1) // 128) * 128
+    scale = HDIM ** (-0.5)
+    slots = n_ex * cap
     everything = []
 
-    def go(copies):
-        for copy in copies:
+    def go(pairs):
+        copies = []
+        for source, target, device in pairs:
+            at = len(everything)
+            copy = remote(source, target, r["send"].at[at], r["recv"].at[at], device)
             copy.start()
-        everything.extend(copies)
+            everything.append(copy)
+            copies.append(copy)
         return copies
 
-    first = go(
-        [remote(sg, ba.at[col], bs.at[i], br.at[i], {"col": p}) for i, p in enumerate(col_peers)]
-    )
-    ba[col] = sg[...]
-    count, width = xn.shape
-    group = k.shape[1]
-    span = lines.shape[2]
-    half = width // 2
-    scale = HDIM ** (-0.5)
-    same = seg_q[...] == seg_k[...]
+    def dot(a, b, how=(((1,), (0,)), ((), ())), precision=None):
+        return lax.dot_general(a, b, how, precision=precision, preferred_element_type=f32)
+
+    greet([mate] + [{"col": p} for p in col_peers] + [{"ex": p} for p in ex_peers])
+    tokens, qkv_w, out_w = r["tokens"], r["qkv_weight"], r["out_weight"]
+    w_in, w_out = r["expert_in"], r["expert_out"]
+    tf, qkvw, outw = r["tf"], r["qkvw"], r["outw"]
+    own_t = tf.at[pl.ds(pl.multiple_of(row * count, count), count)]
+    own_w = qkvw.at[pl.ds(pl.multiple_of(row * half, half), half)]
+    own_o = outw.at[:, pl.ds(pl.multiple_of(row * half, half), half)]
+    entry = go([(tokens, own_t, mate), (qkv_w, own_w, mate), (out_w, own_o, mate)])
+    weights = go([(w_in.at[0], r["p_in"], mate), (w_out.at[0], r["p_out"], mate)])
+    own_t[...] = tokens[...]
+    own_w[...] = qkv_w[...]
+    own_o[...] = out_w[...]
+    gain1, gain2 = r["gain1"][...], r["gain2"][...]
+
+    place = lax.broadcasted_iota(jnp.int32, (span, 128), 0)
+    shift = jnp.where(place < group, place, place - span) - row * count
+    rows_t = (
+        bucket_of(shift, buckets) == lax.broadcasted_iota(jnp.int32, (span, 128), 1)
+    ).astype(f32)
+    r["rows_t"][...] = rows_t
+    lines = dot(r["table"][...], rows_t, INNER, HIGH)
+    lengths = r["lengths"][...]
+    own = lax.broadcasted_iota(jnp.int32, (count, 1), 0) + row * count
+    all_keys = lax.broadcasted_iota(jnp.int32, (1, group), 1)
+    seg_q = jnp.zeros((count, 1), jnp.int32)
+    seg_k = jnp.zeros((1, group), jnp.int32)
+    end = jnp.zeros((1, 1), jnp.int32)
+    for s in range(lengths.shape[1]):
+        end = end + lengths[:, s : s + 1]
+        seg_q = seg_q + (own >= end).astype(jnp.int32)
+        seg_k = seg_k + (all_keys >= end).astype(jnp.int32)
+    same = seg_q == seg_k
+
+    def normed(block):
+        wide = block.astype(f32)
+        inverse = lax.rsqrt(jnp.mean(wide * wide, axis=1, keepdims=True) + EPS)
+        return wide * inverse, inverse
+
+    entry[0].wait_recv()
+    r["xn"][...] = (normed(tf[...])[0] * gain1).astype(bf16)
+    entry[1].wait_recv()
+    r["qkv"][...] = dot(r["xn"][...], qkvw[...]).astype(bf16)
+    mine = r["qkv"][pl.ds(pl.multiple_of(row * count, count), count), :]
+    mixed = []
     for h in range(heads):
-        raw = lax.dot_general(q[h], k[h], INNER, preferred_element_type=f32)
-        raw = raw * scale + bias_of(lines[h], count, group)
-        prob_s[h] = jnp.exp(jnp.where(same, raw, NEG) - level[h])
-    for copy in first:
+        at = h * tri
+        r["q"][h] = mine[:, at : at + HDIM]
+        r["k"][h] = r["qkv"][:, at + HDIM : at + 2 * HDIM]
+        r["v"][h] = r["qkv"][:, at + 2 * HDIM : at + 3 * HDIM]
+        raw = dot(r["q"][h], r["k"][h], INNER)
+        raw = raw * scale + bias_of(lines[h : h + 1], count, group)
+        raw = jnp.where(same, raw, NEG)
+        expo = jnp.exp(raw - jnp.max(raw, axis=1, keepdims=True))
+        prob = expo / jnp.sum(expo, axis=1, keepdims=True)
+        r["prob"][h] = prob
+        mixed.append(dot(prob.astype(bf16), r["v"][h]))
+    r["attn"][...] = jnp.concatenate(mixed, axis=1).astype(bf16)
+    entry[2].wait_recv()
+    r["bb"][...] = dot(r["attn"][...], outw[...]).astype(bf16).reshape(n_col, quarter, width)
+    copies = go([(r["bb"].at[p], r["bl"].at[i], {"col": p}) for i, p in enumerate(col_peers)])
+    here = pl.ds(pl.multiple_of(col * quarter, quarter), quarter)
+    put = (
+        lax.broadcasted_iota(jnp.int32, (slots, quarter), 0) == r["place"][col]
+    ).astype(f32)
+    owner = lax.broadcasted_iota(jnp.int32, (slots, n_ex), 0)
+    kind = lax.broadcasted_iota(jnp.int32, (slots, n_ex), 1) * cap
+    owner = ((owner >= kind) & (owner < kind + cap)).astype(f32)
+    picks = dot(put, owner, OUTER)
+    put = put.astype(bf16)
+    upstream = r["cotangent"][here, :].astype(f32)
+    state = tokens[here, :].astype(f32) + r["bb"][col].astype(f32)
+    for i, copy in enumerate(copies):
+        copy.wait_recv()
+        state = state + r["bl"][i].astype(f32)
+    unit2, inv2 = normed(state)
+    xn2 = (unit2 * gain2).astype(bf16)
+    logits = dot(xn2, r["router"][...])
+    raised = jnp.exp(logits - jnp.max(logits, axis=1, keepdims=True))
+    gates = raised / jnp.sum(raised, axis=1, keepdims=True)
+    gate = jnp.sum(gates * picks, axis=1, keepdims=True)
+    outb = r["outb"]
+    outb[:, :cap, :] = dot(put, xn2).astype(bf16).reshape(n_ex, cap, width)
+    scaled = (gate * upstream).astype(bf16)
+    outb[:, cap:, :] = dot(put, scaled).astype(bf16).reshape(n_ex, cap, width)
+
+    land = r["land"]
+    first = go([(outb.at[p], land.at[col, ex], {"ex": p}) for p in ex_peers])
+    land[col, ex] = outb[ex]
+    spread = go([(land.at[col, ex], land.at[col, ex], {"col": p}) for p in col_peers])
+    for i, copy in enumerate(first):
+        copy.wait_recv()
+        slot = lax.rem(ex + n_ex - 1 - i, n_ex)
+        spread += go([(land.at[col, slot], land.at[col, slot], {"col": p}) for p in col_peers])
+    for copy in weights + spread:
+        copy.wait_recv()
+    many = n_col * n_ex * cap
+    x = land[:, :, :cap, :].reshape(many, width)
+    g = land[:, :, cap:, :].reshape(many, width)
+    y = jnp.zeros((many, width), f32)
+    d = jnp.zeros((many, width), f32)
+    kept = []
+    for wi, wo in ((w_in[0], w_out[0]), (r["p_in"][...], r["p_out"][...])):
+        value, slope = gelu_parts(dot(x, wi))
+        hid = value.astype(bf16)
+        y = y + dot(hid, wo)
+        d_pre = (dot(g, wo, INNER) * slope).astype(bf16)
+        d = d + dot(d_pre, wi, INNER)
+        kept.append((hid, d_pre))
+    part = r["part"]
+    part[:, :, :cap, :] = y.astype(bf16).reshape(n_col, n_ex, cap, width)
+    part[:, :, cap:, :] = d.astype(bf16).reshape(n_col, n_ex, cap, width)
+    sums = go([(part.at[p], r["got"].at[i], {"col": p}) for i, p in enumerate(col_peers)])
+    r["s_in"][...] = dot(x, kept[1][1], OUTER).astype(bf16)
+    r["s_out"][...] = dot(kept[1][0], g, OUTER).astype(bf16)
+    grads = go([(r["s_in"], r["r_in"], mate), (r["s_out"], r["r_out"], mate)])
+    r["g_in"][0] = dot(x, kept[0][1], OUTER)
+    r["g_out"][0] = dot(kept[0][0], g, OUTER)
+    total = part[col].astype(f32)
+    for i, copy in enumerate(sums):
+        copy.wait_recv()
+        total = total + r["got"][i].astype(f32)
+    r["summed"][...] = total.astype(bf16)
+    back = r["back"]
+    home = go([(r["summed"].at[p], back.at[ex], {"ex": p}) for p in ex_peers])
+    back[ex] = r["summed"][ex]
+    unit, inv1 = normed(tokens[...])
+    r["unit"][...] = unit
+    for copy in home:
+        copy.wait_recv()
+
+    expert_y = dot(put, back[:, :cap, :].reshape(slots, width), OUTER)
+    d_entry = dot(put, back[:, cap:, :].reshape(slots, width), OUTER)
+    r["output"][...] = state + gate * expert_y
+    d_gate = jnp.sum(upstream * expert_y, axis=1, keepdims=True)
+    d_logits = gates * (picks * d_gate - gate * d_gate)
+    d_xn2 = dot(d_logits, r["router"][...].astype(f32), INNER, HIGH) + d_entry
+    u2 = gain2 * d_xn2
+    d_state = upstream + inv2 * (u2 - unit2 * jnp.mean(u2 * unit2, axis=1, keepdims=True))
+    r["ds"][...] = d_state
+    ba = r["ba"]
+    ba[col] = d_state.astype(bf16)
+    copies = go([(ba.at[col], ba.at[col], {"col": p}) for p in col_peers])
+    sa = r["sa"]
+    sa[...] = jnp.zeros(sa.shape, f32)
+    sa[1:2, :width] = jnp.sum(d_xn2 * unit2, axis=0, keepdims=True)
+    sa[2 : 2 + n_ex, :width] = dot(d_logits, xn2.astype(f32), OUTER, HIGH)
+    for copy in grads:
+        copy.wait_recv()
+    r["g_in"][0] += r["r_in"][...].astype(f32)
+    r["g_out"][0] += r["r_out"][...].astype(f32)
+    for copy in copies:
         copy.wait_recv()
     branch = ba[...].reshape(count, width)
-    d_attn = lax.dot_general(branch, outw[...], INNER, preferred_element_type=f32).astype(bf16)
-    out_full = lax.dot_general(attn[...], branch, OUTER, preferred_element_type=f32).astype(bf16)
-    ob[0] = out_full[:, :half]
-    ob[1] = out_full[:, half:]
-    out_one = go([remote(ob.at[1 - row], ol, os1.at[0], or1.at[0], mate)])
-
+    d_attn = dot(branch, outw[...], INNER).astype(bf16)
+    kvb, kvl, st, tb, tl = r["kvb"], r["kvl"], r["st"], r["tb"], r["tl"]
+    qs, qx, qf = r["qs"], r["qx"], r["qf"]
+    ob, ol, os_, ox, of_ = r["ob"], r["ol"], r["os"], r["ox"], r["of"]
+    own_xn = r["xn"][pl.ds(pl.multiple_of(row * count, count), count), :]
     d_query, diags, kv_copies, t_copies, q_copies, a_copies = {}, [], {}, {}, {}, {}
 
     def head(h):
-        prob = prob_s[h]
-        g = d_attn[:, h * HDIM : (h + 1) * HDIM]
-        d_prob = lax.dot_general(g, v[h], INNER, preferred_element_type=f32)
+        prob = r["prob"][h]
+        grad = d_attn[:, h * HDIM : (h + 1) * HDIM]
+        d_prob = dot(grad, r["v"][h], INNER)
         mean = jnp.sum(d_prob * prob, axis=1, keepdims=True)
         ds = (prob * (d_prob - mean)).astype(bf16)
-        d_key = lax.dot_general(ds, q[h], OUTER, preferred_element_type=f32) * scale
-        d_val = lax.dot_general(prob.astype(bf16), g, OUTER, preferred_element_type=f32)
+        d_key = dot(ds, r["q"][h], OUTER) * scale
+        d_val = dot(prob.astype(bf16), grad, OUTER)
         kvb[h] = (
             jnp.concatenate([d_key, d_val], axis=1).astype(bf16).reshape(2, count, 2 * HDIM)
         )
-        kv_copies[h] = go([remote(kvb.at[h, 1 - row], kvl.at[h], ks.at[h], kr.at[h], mate)])
-        d_query[h] = jnp.dot(ds, k[h], preferred_element_type=f32) * scale
-        diags.append(diagonals_of(ds.astype(f32), span))
+        kv_copies[h] = go([(kvb.at[h, 1 - row], kvl.at[h], mate)])
+        d_query[h] = dot(ds, r["k"][h]) * scale
+        r["dsc"][h] = ds
 
     def finish(h):
         kv_copies[h][0].wait_recv()
         pair = kvb[h, row].astype(f32) + kvl[h].astype(f32)
         rows = jnp.concatenate([d_query[h], pair], axis=1).astype(bf16)
         st[h] = rows
-        full = lax.dot_general(rows, xn[...], OUTER, preferred_element_type=f32).astype(bf16)
+        full = dot(rows, own_xn, OUTER).astype(bf16)
         tb[h, 0] = full[:, :half]
         tb[h, 1] = full[:, half:]
-        t_copies[h] = go([remote(tb.at[h, 1 - row], tl.at[h], ts.at[h], tr.at[h], mate)])
+        t_copies[h] = go([(tb.at[h, 1 - row], tl.at[h], mate)])
 
     def second(h):
         t_copies[h][0].wait_recv()
         both = tb[h, row].astype(f32) + tl[h].astype(f32)
         qs[h] = both.astype(bf16).reshape(qs.shape[1:])
         q_copies[h] = go(
-            [
-                remote(qs.at[h, p], qx.at[h, i], qss.at[h, i], qsr.at[h, i], {"ex": p})
-                for i, p in enumerate(ex_peers)
-            ]
+            [(qs.at[h, p], qx.at[h, i], {"ex": p}) for i, p in enumerate(ex_peers)]
         )
 
     def third(h):
@@ -425,165 +430,164 @@
             copy.wait_recv()
             total = total + qx[h, i].astype(f32)
         qf[h, ex] = total.astype(bf16)
-        a_copies[h] = go(
-            [
-                remote(qf.at[h, ex], qf.at[h, ex], qas.at[h, i], qar.at[h, i], {"ex": p})
-                for i, p in enumerate(ex_peers)
-            ]
-        )
+        a_copies[h] = go([(qf.at[h, ex], qf.at[h, ex], {"ex": p}) for p in ex_peers])
 
     head(0)
+    out_full = dot(r["attn"][...], branch, OUTER).astype(bf16)
+    ob[0] = out_full[:, :half]
+    ob[1] = out_full[:, half:]
+    out_one = go([(ob.at[1 - row], ol, mate)])
+    finish(0)
     for h in range(1, heads):
         head(h)
-        if h >= 2:
-            second(h - 2)
-        finish(h - 1)
+        second(h - 1)
+        finish(h)
         if h == 1:
             out_one[0].wait_recv()
             both = ob[row].astype(f32) + ol[...].astype(f32)
             os_[...] = both.astype(bf16).reshape(os_.shape)
-            out_two = go(
-                [
-                    remote(os_.at[p], ox.at[i], os2.at[i], or2.at[i], {"ex": p})
-                    for i, p in enumerate(ex_peers)
-                ]
-            )
-    finish(heads - 1)
-    second(heads - 2)
+            out_two = go([(os_.at[p], ox.at[i], {"ex": p}) for i, p in enumerate(ex_peers)])
     rows = jnp.concatenate([st[h] for h in range(heads)], axis=1)
-    d_xn = lax.dot_general(rows, qkvw[...], INNER, preferred_element_type=f32)
+    d_xn = dot(rows, qkvw[...], INNER)
+    xb, xl = r["xb"], r["xl"]
     xb[...] = d_xn.astype(bf16).reshape(xb.shape)
-    x_copies = go(
-        [remote(xb.at[p], xl.at[i], xs.at[i], xr.at[i], {"col": p}) for i, p in enumerate(col_peers)]
-    )
+    x_copies = go([(xb.at[p], xl.at[i], {"col": p}) for i, p in enumerate(col_peers)])
     second(heads - 1)
-    norm = jnp.sum(d_xn * unit[...], axis=0, keepdims=True)
+    diags = [diagonals_of(r["dsc"][h].astype(f32), span) for h in range(heads)]
     diag = jnp.concatenate(diags + [jnp.zeros((8 - heads, span), f32)], axis=0)
-    table = jnp.dot(diag, rows_t[...], precision=HIGH, preferred_element_type=f32)
-    spot = lax.broadcasted_iota(jnp.int32, small.shape, 0)
-    sa[:, :width] = jnp.where(spot == 0, norm, small[...])
-    sa[:, width:] = table
-    small_one = go([remote(sa, sl, ss1.at[0], sr1.at[0], mate)])
+    sa[:1, :width] = jnp.sum(d_xn * r["unit"][...], axis=0, keepdims=True)
+    sa[:, width:] = dot(diag, r["rows_t"][...], precision=HIGH)
+    sb = r["sb"]
+    small_one = go([(sa, r["sl"], mate)])
     third(0)
     small_one[0].wait_recv()
-    sb[0] = sa[...] + sl[...]
-    small_two = go(
-        [
-            remote(sb.at[0], sx.at[i], ss2.at[i], sr2.at[i], {"ex": p})
-            for i, p in enumerate(ex_peers)
-        ]
-    )
+    sb[0] = sa[...] + r["sl"][...]
+    small_two = go([(sb.at[0], r["sx"].at[i], {"ex": p}) for i, p in enumerate(ex_peers)])
+    third(1)
     total = os_[ex].astype(f32)
     for i, copy in enumerate(out_two):
         copy.wait_recv()
         total = total + ox[i].astype(f32)
     of_[ex] = total.astype(bf16)
-    out_three = go(
-        [
-            remote(of_.at[ex], of_.at[ex], os3.at[i], or3.at[i], {"ex": p})
-            for i, p in enumerate(ex_peers)
-        ]
-    )
-    third(1)
+    out_three = go([(of_.at[ex], of_.at[ex], {"ex": p}) for p in ex_peers])
+    for h in range(2, heads):
+        third(h)
     d_own = xb[col].astype(f32)
     for i, copy in enumerate(x_copies):
         copy.wait_recv()
         d_own = d_own + xl[i].astype(f32)
-    scaled = gain[...] * d_own
-    inner = jnp.sum(scaled * unit_q[...], axis=1, keepdims=True) * (1.0 / width)
-    input_o[...] = sgf[...] + inv_q[...] * (scaled - unit_q[...] * inner)
-    for h in range(2, heads):
-        third(h)
+    unit_q, inv_q = normed(tokens[here, :])
+    u1 = gain1 * d_own
+    inner = jnp.mean(u1 * unit_q, axis=1, keepdims=True)
+    r["input_grad"][...] = r["ds"][...] + inv_q * (u1 - unit_q * inner)
     total = sb[0]
     for i, copy in enumerate(small_two):
         copy.wait_recv()
-        total = total + sx[i]
+        total = total + r["sx"][i]
     sb[1] = total
-    small_three = go(
-        [
-            remote(sb.at[1], sc.at[i], ss3.at[i], sr3.at[i], {"col": p})
-            for i, p in enumerate(col_peers)
-        ]
-    )
-    for copy in out_three:
-        copy.wait_recv()
-    out_o[...] = of_[...].astype(f32).reshape(out_o.shape)
-    for i, copy in enumerate(small_three):
-        copy.wait_recv()
-        total = total + sc[i]
-    small_o[:, :width] = total[:, :width]
-    small_o[:, width:] = sb[1, :, width:]
+    small_three = go([(sb.at[1], r["sc"].at[i], {"col": p}) for i, p in enumerate(col_peers)])
     for h in range(heads):
         for copy in a_copies[h]:
             copy.wait_recv()
-        piece = qf[h].astype(f32).reshape(3 * HDIM, half)
-        qkv_o[:, h * 3 * HDIM : (h + 1) * 3 * HDIM] = piece.T
+        piece = qf[h].astype(f32).reshape(tri, half)
+        r["qkv_grad"][:, h * tri : (h + 1) * tri] = piece.T
+    for copy in out_three:
+        copy.wait_recv()
+    r["out_grad"][...] = of_[...].astype(f32).reshape(r["out_grad"].shape)
+    total = sb[1]
+    for i, copy in enumerate(small_three):
+        copy.wait_recv()
+        total = total + r["sc"][i]
+    r["small"][:, :width] = total[:, :width]
+    r["small"][:, width:] = sb[1, :, width:]
     for copy in everything:
         copy.wait_send()
 
 
-def back_block(sg, sgf, attn, outw, q, k, v, level, lines, seg_q, seg_k, xn, unit, qkvw, small,
-               rows_t, unit_q, inv_q, gain):
+def whole_block(buckets, heads, cap, **arrays):
     n_ex, n_col = lax.axis_size("ex"), lax.axis_size("col")
     bf16, f32 = jnp.bfloat16, jnp.float32
-    heads, group, _ = k.shape
-    count, width = xn.shape
-    quarter = sg.shape[0]
-    half = width // 2
-    tri = 3 * HDIM
-    wide = width + rows_t.shape[1]
-    head_rows = outw.shape[0]
-    args = (sg, sgf, attn, outw, q, k, v, level, lines, seg_q, seg_k, xn, unit, qkvw, small,
-            rows_t, unit_q, inv_q, gain)
-    V = pltpu.VMEM
+    count, width = arrays["tokens"].shape
+    quarter = count // n_col
+    group, half, tri = 2 * count, width // 2, 3 * HDIM
+    span = -(-(count + group - 1) // 128) * 128
+    cols = arrays["expert_in"].shape[2]
+    hr = arrays["out_weight"].shape[0]
+    wide = width + 128
+    outs = {
+        "output": (quarter, width),
+        "input_grad": (quarter, width),
+        "qkv_grad": (half, heads * tri),
+        "out_grad": (hr, half),
+        "small": (8, wide),
+        "g_in": (1, width, cols),
+        "g_out": (1, cols, width),
+    }
+    narrow = {
+        "tf": (group, width),
+        "qkvw": (width, heads * tri),
+        "outw": (hr, width),
+        "p_in": (width, cols),
+        "p_out": (cols, width),
+        "xn": (group, width),
+        "qkv": (group, heads * tri),
+        "q": (heads, count, HDIM),
+        "k": (heads, group, HDIM),
+        "v": (heads, group, HDIM),
+        "attn": (count, hr),
+        "bb": (n_col, quarter, width),
+        "bl": (n_col - 1, quarter, width),
+        "outb": (n_ex, 2 * cap, width),
+        "land": (n_col, n_ex, 2 * cap, width),
+        "part": (n_col, n_ex, 2 * cap, width),
+        "got": (n_col - 1, n_ex, 2 * cap, width),
+        "summed": (n_ex, 2 * cap, width),
+        "back": (n_ex, 2 * cap, width),
+        "s_in": (width, cols),
+        "s_out": (cols, width),
+        "r_in": (width, cols),
+        "r_out": (cols, width),
+        "ba": (n_col, quarter, width),
+        "dsc": (heads, count, group),
+        "kvb": (heads, 2, count, 2 * HDIM),
+        "kvl": (heads, count, 2 * HDIM),
+        "st": (heads, count, tri),
+        "tb": (heads, 2, tri, half),
+        "tl": (heads, tri, half),
+        "qs": (heads, n_ex, tri // n_ex, half),
+        "qx": (heads, n_ex - 1, tri // n_ex, half),
+        "qf": (heads, n_ex, tri // n_ex, half),
+        "ob": (2, hr, half),
+        "ol": (hr, half),
+        "os": (n_ex, hr // n_ex, half),
+        "ox": (n_ex - 1, hr // n_ex, half),
+        "of": (n_ex, hr // n_ex, half),
+        "xb": (n_col, quarter, width),
+        "xl": (n_col - 1, quarter, width),
+    }
+    full = {
+        "rows_t": (span, 128),
+        "prob": (heads, count, group),
+        "unit": (count, width),
+        "ds": (quarter, width),
+        "sa": (8, wide),
+        "sl": (8, wide),
+        "sx": (n_ex - 1, 8, wide),
+        "sb": (2, 8, wide),
+        "sc": (n_col - 1, 8, wide),
+    }
+    names = [*arrays, *outs, *narrow, *full, "send", "recv"]
+    dims = (n_ex, n_col, heads, cap, buckets, count, width, quarter)
     return pl.pallas_call(
-        lambda *refs: back_kernel(n_ex, n_col, heads, *refs),
-        out_shape=(
-            jax.ShapeDtypeStruct((quarter, width), f32),
-            jax.ShapeDtypeStruct((half, heads * tri), f32),
-            jax.ShapeDtypeStruct((head_rows, half), f32),
-            jax.ShapeDtypeStruct((8, wide), f32),
-        ),
-        in_specs=[VMEM] * len(args),
-        out_specs=(VMEM,) * 4,
-        scratch_shapes=[
-            V((n_col, quarter, width), bf16),
-            V((heads, count, group), f32),
-            V((heads, 2, count, 2 * HDIM), bf16),
-            V((heads, count, 2 * HDIM), bf16),
-            V((heads, count, tri), bf16),
-            V((heads, 2, tri, half), bf16),
-            V((heads, tri, half), bf16),
-            V((heads, n_ex, tri // n_ex, half), bf16),
-            V((heads, n_ex - 1, tri // n_ex, half), bf16),
-            V((heads, n_ex, tri // n_ex, half), bf16),
-            V((2, head_rows, half), bf16),
-            V((head_rows, half), bf16),
-            V((n_ex, head_rows // n_ex, half), bf16),
-            V((n_ex - 1, head_rows // n_ex, half), bf16),
-            V((n_ex, head_rows // n_ex, half), bf16),
-            V((n_col, quarter, width), bf16),
-            V((n_col - 1, quarter, width), bf16),
-            V((8, wide), f32),
-            V((8, wide), f32),
-            V((n_ex - 1, 8, wide), f32),
-            V((2, 8, wide), f32),
-            V((n_col - 1, 8, wide), f32),
-            DMA((n_col - 1,)), DMA((n_col - 1,)),
-            DMA((heads,)), DMA((heads,)),
-            DMA((heads,)), DMA((heads,)),
-            DMA((heads, n_ex - 1)), DMA((heads, n_ex - 1)),
-            DMA((heads, n_ex - 1)), DMA((heads, n_ex - 1)),
-            DMA((1,)), DMA((1,)),
-            DMA((n_ex - 1,)), DMA((n_ex - 1,)),
-            DMA((n_ex - 1,)), DMA((n_ex - 1,)),
-            DMA((n_col - 1,)), DMA((n_col - 1,)),
-            DMA((1,)), DMA((1,)),
-            DMA((n_ex - 1,)), DMA((n_ex - 1,)),
-            DMA((n_col - 1,)), DMA((n_col - 1,)),
-        ],
+        lambda *refs: whole_kernel(dims, names, *refs),
+        out_shape=tuple(jax.ShapeDtypeStruct(shape, f32) for shape in outs.values()),
+        in_specs=[VMEM] * len(arrays),
+        out_specs=(VMEM,) * len(outs),
+        scratch_shapes=[pltpu.VMEM(shape, bf16) for shape in narrow.values()]
+        + [pltpu.VMEM(shape, f32) for shape in full.values()]
+        + [DMA((96,)), DMA((96,))],
         compiler_params=params(8),
-    )(*args)
+    )(*arrays.values())
 
 
 def expert_exchange(outbound, w_in, w_out):
@@ -637,7 +641,38 @@
     heads = out_weight.shape[0] // HDIM
     buckets = bias_table.shape[0]
     scale = HDIM ** (-0.5)
-    direct = cap % 16 == 0
+    if cap % 16 == 0:
+        place = (routes * cap + slots).reshape(n_col, 1, dispatch_mask)
+        table = jnp.pad(bias_table.T, ((0, 8 - heads), (0, 128 - buckets)))
+        output, input_grad, qkv_grad, out_grad, small, inner_grad, outer_grad = whole_block(
+            buckets,
+            heads,
+            cap,
+            tokens=tokens,
+            qkv_weight=qkv_weight,
+            out_weight=out_weight,
+            table=table,
+            gain1=first_norm_scale[None, :],
+            gain2=second_norm_scale[None, :],
+            router=router_weight,
+            expert_in=expert_in,
+            expert_out=expert_out,
+            lengths=lengths,
+            place=place,
+            cotangent=cotangent,
+        )
+        return (
+            output,
+            input_grad,
+            qkv_grad,
+            out_grad,
+            small[:heads, width : width + buckets].T,
+            small[0, :width],
+            small[1, :width],
+            small[2 : 2 + experts, :width].T,
+            inner_grad,
+            outer_grad,
+        )
     qkv_rows, out_rows, group_tokens = gather_row(qkv_weight, out_weight, tokens)
     group = group_tokens.shape[0]
     local_offset = my_row * tokens_per_device
@@ -729,10 +764,7 @@
         ],
         axis=1,
     )
-    if direct:
-        back, inner_grad, outer_grad = expert_block(outbound, expert_in[0], expert_out[0])
-    else:
-        back, inner_grad, outer_grad = expert_exchange(outbound, expert_in[0], expert_out[0])
+    back, inner_grad, outer_grad = expert_exchange(outbound, expert_in[0], expert_out[0])
     expert_back_rows, entry_back = (
         lax.dot_general(
             put, rows.reshape(experts * cap, width), OUTER, preferred_element_type=jnp.float32
@@ -763,47 +795,6 @@
     inv_quarter = lax.dynamic_slice_in_dim(
         first_inverse_norm, local_offset + quarter_offset, dispatch_mask, 0
     )
-    if direct:
-        small = jnp.concatenate(
-            [jnp.zeros((1, width), jnp.float32), second_norm_slice[None], router_part.T], axis=0
-        )
-        small = jnp.pad(small, ((0, 8 - small.shape[0]), (0, 0)))
-        input_grad, qkv_grad, out_grad, small = back_block(
-            state_grad.astype(jnp.bfloat16),
-            state_grad,
-            attn,
-            out_rows,
-            queries,
-            keys,
-            values,
-            log_total,
-            bias_lines[:, None, :],
-            own_segment[:, None],
-            segment[None, :],
-            xn_own,
-            local_unit_input,
-            qkv_rows,
-            small,
-            jnp.pad(table_rows, ((0, 0), (0, 128 - buckets))),
-            quarter_unit_input,
-            inv_quarter,
-            first_norm_scale[None, :],
-        )
-        norm1_grad, norm2_grad = small[0, :width], small[1, :width]
-        router_grad = small[2 : 2 + experts, :width].T
-        table_grad = small[:heads, width : width + buckets].T
-        return (
-            output,
-            input_grad,
-            qkv_grad,
-            out_grad,
-            table_grad,
-            norm1_grad,
-            norm2_grad,
-            router_grad,
-            inner_grad[None],
-            outer_grad[None],
-        )
     branch_all = gather_blocks(state_grad.astype(jnp.bfloat16), "col", 5).reshape(
         tokens_per_device, width
     )

time: 131 us -> 105 us (0.80)
  local copies, waits for them, and re-layouts: 31.5 us -> 18.6 us
  matrix products: 9.59 us -> 0 us
  other arithmetic: 5.7 us -> 0.76 us
  Pallas kernels: 82 us -> 84.6 us
    dot_general x16 -> x0, matrix products: 9.59 us -> none  [the longest x3 3.34 us: scores_of(): jnp.einsum('qd,kd->qk', query, key, preferred_element_type=jnp.float32)]
    dynamic_slice x9 -> x0, local copies, waits for them, and re-layouts: 5.52 us -> none  [the longest x2 2.61 us: on_device(): lax.dynamic_slice_in_dim(first_inverse_norm, local_offset + quarter_offse...]
    unnamed x68 -> x34, local copies, waits for them, and re-layouts: 18.1 us -> 14.7 us
    pallas_call x4 -> x1, Pallas kernels: 82 us -> 84.6 us  [whole_block(): pl.pallas_call(lambda *refs: whole_kernel(dims, names, *refs), out_shape=...]
    reduce_sum x8 -> x0, other arithmetic: 1.99 us -> none  [the longest x1 1.01 us: on_device(): jnp.mean(hidden_state * hidden_state, axis=1, keepdims=True) + EPS]
    reshape x4 -> x1, local copies, waits for them, and re-layouts: 2.03 us -> 0.09 us  [on_device(): place = (routes * cap + slots).reshape(n_col, 1, dispatch_mask)]
    convert_element_type x2 -> x0, other arithmetic: 1.89 us -> none  [the longest x1 1.81 us: on_device(): state_grad.astype(jnp.bfloat16)]
where the time goes in v3:
time: 105 us
  Pallas kernels  84.6 us (81%)
  local copies, waits for them, and re-layouts  18.6 us (18%)
    pallas_call x1, Pallas kernels, whole_block(): pl.pallas_call(lambda *refs: whole_kernel(dims, names, *refs), out_shape=...  84.6 us
    unnamed x34, local copies, waits for them, and re-layouts  14.7 us

profile of v3, /device:TPU:0, one launch (start us, length us, event | category | flops | bytes accessed | tf_op | source)
XLA Modules:
  0.0 104.8 jit_solution(6847881328289128476)
XLA Ops:
  0.6 0.0 copy-start
  0.7 0.8 multiply_add_fusion
  1.4 0.1 reshape.23.refs_10_
  1.5 0.7 broadcast_in_dim.6.refs_4_
  2.2 0.7 broadcast_in_dim.7.refs_5_
  2.9 0.7 pad.4.refs_3_
  3.6 0.9 copy.24.refs_6_
  4.4 1.3 %copy.23.refs_1_ = bf16[384,576]{1,0:T(8,128)(2,1)S(1)} copy(bf16[384,576]{0,1:T(8,128)(2,1)} %param.14) | data formatting | bytes 884736 | tf_op args[1]
  5.7 0.0 copy-done
  5.7 0.0 copy-start.1
  5.7 1.1 %copy-done.1 = bf16[1,384,768]{2,1,0:T(8,128)(2,1)S(1)} copy-done((bf16[1,384,768]{2,1,0:T(8,128)(2,1)S(1)}, bf16[1,384,768]{2,1,0:T(8,128)(2,1)}, u32[]{:S(2)}) %copy-start.1) | copy-done | bytes 589848
  6.8 0.0 copy-start.4
  6.8 1.0 copy-done.4
  7.7 0.0 copy-start.5
  7.7 1.0 copy-done.5
  8.7 0.0 copy-start.6
  8.7 0.9 copy-done.6
  9.6 0.0 copy-start.11
  9.6 0.7 copy-done.11
  10.3 84.6 %shard_map.204 = (f32[48,768]{1,0:T(8,128)S(1)}, f32[48,768]{1,0:T(8,128)S(1)}, f32[384,576]{1,0:T(8,128)S(1)}, f32[192,384]{1,0:T(8,128)S(1)}, f32[8,896]{1,0:T...) custom-call(bf16[192,768]{1,0:T(8,128)(2,1)S(1)} %copy-done.4, bf16[384,576]{1,0:T(8,128)(2,1)S(1)} %copy.23.refs_1_, ...), custom_call_target="tpu_custom_call" | custom-call | tf_op jit(solution)/shard_map/pallas_call | solution.py:581
  94.9 0.0 copy-start.2
  94.9 0.7 copy-done.2
  95.6 0.0 copy-start.7
  95.6 0.7 copy-done.7
  96.3 0.0 copy-start.9
  96.3 0.7 copy-done.9
  97.0 0.0 copy-start.10
  97.0 0.0 copy-start.8
  97.0 0.6 slice_bitcast_fusion.1
  97.5 0.6 slice_reduce_fusion
  98.2 0.6 slice_bitcast_fusion
  98.8 0.0 copy-start.3
  98.8 1.2 %copy.25 = f32[384,576]{0,1:T(8,128)} copy(f32[384,576]{1,0:T(8,128)S(1)} %get-tuple-element.26) | data formatting | bytes 1769472
  100.0 0.0 copy-done.10
  100.0 0.7 copy.31
  100.7 0.0 copy-done.8
  100.7 0.7 copy.32
  101.3 0.0 copy-done.3
  101.3 0.7 copy.33
  102.0 0.0 copy-start.12
  102.0 1.0 copy.34
  103.1 0.7 copy-done.12
  103.7 1.0 copy.35
Async XLA Ops:
  0.6 5.1 %copy-start = (bf16[1,768,384]{2,1,0:T(8,128)(2,1)S(1)}, bf16[1,768,384]{2,1,0:T(8,128)(2,1)}, u32[]{:S(2)}) copy-start(bf16[1,768,384]{2,1,0:T(8,128)(2,1)} %refs_7_.1) | copy-start | bytes 1769476
  5.7 1.1 %copy-start.1 = (bf16[1,384,768]{2,1,0:T(8,128)(2,1)S(1)}, bf16[1,384,768]{2,1,0:T(8,128)(2,1)}, u32[]{:S(2)}) copy-start(bf16[1,384,768]{2,1,0:T(8,128)(2,1)} %refs_8_.1) | copy-start | bytes 1769476
  6.8 1.0 copy-start.4
  7.7 1.0 copy-start.5
  8.7 0.9 copy-start.6
  9.6 0.7 copy-start.11
  94.9 0.7 copy-start.2
  95.6 0.7 copy-start.7
  96.3 0.7 copy-start.9
  97.0 3.0 %copy-start.10 = (f32[48,768]{1,0:T(8,128)S(1)}, f32[48,768]{1,0:T(8,128)}, u32[]{:S(2)}) copy-start(f32[48,768]{1,0:T(8,128)} %copy-done.9) | copy-start | bytes 442372
  97.0 3.7 %copy-start.8 = (f32[48,768]{1,0:T(8,128)S(1)}, f32[48,768]{1,0:T(8,128)}, u32[]{:S(2)}) copy-start(f32[48,768]{1,0:T(8,128)} %copy-done.7) | copy-start | bytes 442372
  98.8 2.6 %copy-start.3 = (f32[192,384]{1,0:T(8,128)S(1)}, f32[192,384]{1,0:T(8,128)}, u32[]{:S(2)}) copy-start(f32[192,384]{1,0:T(8,128)} %copy-done.2) | copy-start | bytes 884740
  102.0 1.7 %copy-start.12 = (f32[1,384,768]{2,1,0:T(8,128)S(1)}, f32[1,384,768]{2,1,0:T(8,128)}, u32[]{:S(2)}) copy-start(f32[1,384,768]{2,1,0:T(8,128)} %get-tuple-element.55) | copy-start | bytes 3538948
